TPU v7x, 512 devices: a whole 4x4x16 slice. The times are simulated.
512 devices in a mesh: clip: 32 (over z, core), frame: 16 (over x, y).
Axes of the slice: x: 4, y: 4, z: 16, core: 2. Of those that a mesh axis runs over, the one named last changes fastest.
Arguments:
- inputs: bfloat16 [32, 5, 128, 64, 128], P('clip', None, 'frame'), may hold values from -16 to 16
- norm_gain: float32 [128], replicated, may hold values from 0.1 to 1.9
- norm_bias: float32 [128], replicated, may hold values from -3 to 3
- conv_weight: bfloat16 [3, 3, 3, 128, 128], replicated, may hold values from -0.109375 to 0.109375
- conv_bias: float32 [128], replicated, may hold values from -3 to 3
- down_weight: bfloat16 [3, 3, 128, 128], replicated, may hold values from -0.1875 to 0.1875
- down_bias: float32 [128], replicated, may hold values from -3 to 3
- time_weight: bfloat16 [3, 128, 128], replicated, may hold values from -0.3125 to 0.3125
- time_bias: float32 [128], replicated, may hold values from -3 to 3
- head_weight: bfloat16 [128, 32], replicated, may hold values from -0.5 to 0.5
- head_bias: float32 [32], replicated, may hold values from -3 to 3
- tile_shard: int32 [32, 3, 512], P('clip', None, 'frame'), may hold values from 0 to 31, as said below
- tile_slot: int32 [32, 3, 512], P('clip', None, 'frame'), may hold values from 0 to 1023, as said below
Outputs:
- packed: bfloat16 [3, 32768, 128], P(None, ('clip', 'frame'))
Inputs may be any that keep to these rules, and one draw needn't show every extreme that they name: `tile_shard`: tiles t of one clip and reduced frame with t // 32 = g form block g. In every such block at most 2 tiles go to one shard, and in every reduced frame and block some shard receives exactly 2 tiles from every clip. `tile_slot`: the tiles of block g sent to one shard in one reduced frame have distinct slots from g * 64 to (g + 1) * 64 - 1.
All inputs are finite; a program needn't handle non-finite values.
Results may differ from a plain program's by a relative error of at most 0.006.
Values may be sent and summed in bfloat16 or wider, within the bound.
No kernel may reach another device: no remote copies, remote signals or barrier semaphores. Data moves between devices by JAX's collectives and lax.ppermute only.
A program may use at most 64 MiB of HBM per device.

v0:
```python
import jax
import jax.numpy as jnp
from jax import lax
from jax.sharding import PartitionSpec as P

GROUPS = 32


EPSILON = 1e-06


def with_halo(cells, sides, width):
    for axis, dim in sides:
        count = lax.axis_size(axis)
        ends = count - 1
        head = lax.slice_in_dim(cells, 0, width, axis=dim)
        tail = lax.slice_in_dim(cells, cells.shape[dim] - width, cells.shape[dim], axis=dim)
        cells = jnp.concatenate(
            [
                lax.ppermute(tail, axis, [(i, (i + 1) % count) for i in range(ends)]),
                cells,
                lax.ppermute(head, axis, [((i + 1) % count, i) for i in range(ends)]),
            ],
            axis=dim,
        )
    return cells


def from_behind(block, axis, distance):
    devices = range(lax.axis_size(axis))
    route = [(i - distance, i) for i in devices if i - distance in devices]
    return lax.ppermute(block, axis, route)


def causal_mix(stacked_pad, weight, bias_vec, frame_count, row_count, col_count):
    channels = weight.shape[-1]
    col_stack = jnp.concatenate(
        [stacked_pad[:, :, col_tap : col_tap + col_count] for col_tap in range(3)], axis=-1
    )
    accum_sum = jnp.zeros((frame_count * row_count * col_count, channels), jnp.float32)
    for time_tap in range(3):
        for row_tap in range(3):
            stacked = col_stack[time_tap : time_tap + frame_count, row_tap : row_tap + row_count]
            accum_sum = accum_sum + jnp.dot(
                stacked.reshape(-1, 3 * channels),
                weight[time_tap, row_tap].reshape(3 * channels, channels),
                preferred_element_type=jnp.float32,
            )
    return accum_sum.reshape(frame_count, row_count, col_count, channels) + bias_vec


def strided_mix(padded, weight, bias_vec, row_out, col_out):
    frame_count = padded.shape[0]
    channels = weight.shape[-1]
    accum_sum = jnp.zeros((frame_count * row_out * col_out, channels), jnp.float32)
    for row_tap in range(3):
        window = padded[:, row_tap : row_tap + 2 * row_out : 2]
        stacked = jnp.concatenate(
            [window[:, :, col_tap : col_tap + 2 * col_out : 2] for col_tap in range(3)], axis=-1
        )
        accum_sum = accum_sum + jnp.dot(
            stacked.reshape(-1, 3 * channels),
            weight[row_tap].reshape(3 * channels, channels),
            preferred_element_type=jnp.float32,
        )
    return accum_sum.reshape(frame_count, row_out, col_out, channels) + bias_vec


def time_mix(padded, weight, bias_vec, lat_count):
    channels = weight.shape[-1]
    rest = padded.shape[1:3]
    accum_sum = jnp.zeros((lat_count * rest[0] * rest[1], channels), jnp.float32)
    for time_tap in range(3):
        window = padded[time_tap : time_tap + 2 * lat_count - 1 : 2]
        accum_sum = accum_sum + jnp.dot(
            window.reshape(-1, channels), weight[time_tap], preferred_element_type=jnp.float32
        )
    return accum_sum.reshape(lat_count, rest[0], rest[1], channels) + bias_vec


def project_head(lat_mixed, head_weight, head_bias):
    lat_count, row_count, col_count, channels = lat_mixed.shape
    out_channels = head_weight.shape[1]
    latent = (
        jnp.dot(lat_mixed.reshape(-1, channels), head_weight, preferred_element_type=jnp.float32)
        + head_bias
    )
    return latent.astype(jnp.bfloat16).reshape(lat_count, row_count, col_count, out_channels)


def to_tiles(latent):
    lat_count, row_count, col_count, out_channels = latent.shape
    split_up = latent.reshape(lat_count, row_count // 2, 2, col_count // 2, 2, out_channels)
    split_up = split_up.transpose(0, 1, 3, 2, 4, 5)
    return split_up.reshape(lat_count, row_count // 2 * (col_count // 2), 4 * out_channels)


def normalize(block, group_mean, inverse, norm_gain, norm_bias):
    shape_in = block.shape
    grouped = block.astype(jnp.float32).reshape(shape_in[:-1] + (GROUPS, shape_in[-1] // GROUPS))
    normed = ((grouped - group_mean[:, None]) * inverse[:, None]).reshape(shape_in)
    return jax.nn.silu(normed * norm_gain + norm_bias)


def local(
    inputs,
    norm_gain,
    norm_bias,
    conv_weight,
    conv_bias,
    down_weight,
    down_bias,
    time_weight,
    time_bias,
    head_weight,
    head_bias,
    tile_shard,
    tile_slot,
):
    activations = inputs[0]
    frame_count, row_count, col_count, channels = activations.shape
    frame_devs = lax.axis_size("frame")
    position = lax.axis_index("frame")
    entries = frame_count * frame_devs * row_count * col_count * (channels // GROUPS)
    grouped = activations.reshape(frame_count, row_count, col_count, GROUPS, channels // GROUPS)
    local_sum = jnp.sum(grouped, axis=(0, 1, 2, 4), dtype=jnp.float32)
    group_mean = lax.psum(local_sum, "frame") / entries
    centred = grouped.astype(jnp.float32) - group_mean[:, None]
    group_var = lax.psum(jnp.sum(centred * centred, axis=(0, 1, 2, 4)), "frame") / entries
    inverse = lax.rsqrt(group_var + EPSILON)
    hidden = normalize(activations, group_mean, inverse, norm_gain, norm_bias).astype(jnp.bfloat16)
    hidden_ext = with_halo(hidden, (("frame", 1),), 1)
    hidden_pad = jnp.pad(hidden_ext, ((2, 0), (0, 0), (1, 1), (0, 0)))
    mixed = causal_mix(hidden_pad, conv_weight, conv_bias, frame_count, row_count, col_count)
    with_skip = (activations.astype(jnp.float32) + mixed).astype(jnp.bfloat16)
    following = from_behind(with_skip[:, :1], "frame", -1)
    padded = jnp.pad(
        jnp.concatenate([with_skip, following], axis=1), ((0, 0), (0, 0), (0, 1), (0, 0))
    )
    reduced = strided_mix(padded, down_weight, down_bias, row_count // 2, col_count // 2).astype(
        jnp.bfloat16
    )
    time_pad = jnp.pad(reduced, ((2, 0), (0, 0), (0, 0), (0, 0)))
    lat_mixed = time_mix(time_pad, time_weight, time_bias, (frame_count + 1) // 2).astype(
        jnp.bfloat16
    )
    latent = project_head(lat_mixed, head_weight, head_bias)
    patch_tiles = to_tiles(latent)
    lat_count = patch_tiles.shape[0]
    tile_count = patch_tiles.shape[1]
    tile_width = patch_tiles.shape[2]
    shard_ids = tile_shard[0]
    shards = lax.axis_size("clip")
    pair_slots = 2 * (tile_count // shards)
    slot_block = shards * pair_slots
    slot_ids = tile_slot[0] - position * slot_block
    matches = (shard_ids[:, :, None] == jnp.arange(shards, dtype=jnp.int32)[None, None, :]).astype(
        jnp.int32
    )
    rank_in = jnp.sum((jnp.cumsum(matches, axis=1) - 1) * matches, axis=-1)
    target = shard_ids * pair_slots + rank_in
    chooser = target[:, None, :] == jnp.arange(slot_block, dtype=jnp.int32)[None, :, None]
    outgoing = jnp.einsum(
        "lpt,ltc->lpc",
        chooser.astype(jnp.bfloat16),
        patch_tiles,
        preferred_element_type=jnp.float32,
    ).astype(jnp.bfloat16)
    filled = jnp.any(chooser, axis=-1).astype(jnp.int32)
    out_slot = jnp.sum(jnp.where(chooser, slot_ids[:, None, :], 0), axis=-1) + slot_block * (
        1 - filled
    )
    outgoing = outgoing.reshape(lat_count, shards, pair_slots, tile_width)
    out_slot = out_slot.reshape(lat_count, shards, pair_slots)
    arrived, arrived_slot = (
        lax.all_to_all(outgoing, "clip", split_axis=1, concat_axis=1, tiled=True),
        lax.all_to_all(out_slot, "clip", split_axis=1, concat_axis=1, tiled=True),
    )
    arrived = arrived.reshape(lat_count, slot_block, tile_width)
    arrived_slot = arrived_slot.reshape(lat_count, slot_block)
    placer = (
        arrived_slot[:, None, :] == jnp.arange(slot_block, dtype=jnp.int32)[None, :, None]
    ).astype(jnp.bfloat16)
    packed = jnp.einsum("lqp,lpc->lqc", placer, arrived, preferred_element_type=jnp.float32)
    return packed.astype(jnp.bfloat16)


def solution(mesh):
    placed = (
        P("clip", None, "frame", None, None),
        P(),
        P(),
        P(),
        P(),
        P(),
        P(),
        P(),
        P(),
        P(),
        P(),
        P("clip", None, "frame"),
        P("clip", None, "frame"),
    )
    return jax.shard_map(
        local,
        mesh=mesh,
        in_specs=placed,
        out_specs=P(None, ("clip", "frame"), None),
        check_vma=False,
    )
```

profile of v0, /device:TPU:1, one launch (start us, length us, event | category | flops | bytes accessed | tf_op | source)
XLA Modules:
  0.0 159.8 jit_solution(9977026523880705705)
XLA Ops:
  0.0 1.5 convert_reduce_fusion
  1.7 34.3 %psum.14 = f32[32]{0:T(128)S(1)} all-reduce(f32[32]{0:T(128)S(1)} %reduce_sum.54), channel_id=1, replica_groups=mesh['clip'=32,'frame'=16] {'frame'}, use_global_device_ids=true, to_apply=%region_6.7 | all-reduce | flops 32 | bytes 256 | tf_op jit(solution)/shard_map/psum | solution.py:127
  36.2 1.5 fusion.20
  37.9 28.5 %psum.15 = f32[32]{0:T(128)S(1)} all-reduce(f32[32]{0:T(128)S(1)} %reduce_sum.57), channel_id=1, replica_groups=mesh['clip'=32,'frame'=16] {'frame'}, use_global_device_ids=true, to_apply=%region_9.10 | all-reduce | flops 32 | bytes 256 | tf_op jit(solution)/shard_map/psum | solution.py:129
  67.2 3.4 %collective-permute-start = (bf16[5,1,64,128]{3,2,1,0:T(8,128)(2,1)S(1)}, bf16[5,1,64,128]{3,2,1,0:T(8,128)(2,1)S(1)}, u32[]{:S(2)}, u32[]{:S(2)}) collective-permute-start(bf16[5,1,64,128]{3,2,1,0:T(8,128)(2,1)S(1)} %get-tuple-element.29), channel_id=1, source_target_pairs={{0,1},{1,2},{2,3},{3,4},{4,5},{5,6},{6,7},{7,8},{8,9},{9,10},{10,1... | collective-permute-start | bytes 245768 | tf_op jit(solution)/shard_map/ppermute | solution.py:20
  70.6 1.3 collective-permute-start.1
  72.5 0.7 copy.24
  73.2 30.7 %all-to-all-start = ((s32[3,32,2]{0,2,1:T(2,128)}), s32[3,32,2]{0,2,1:T(2,128)S(1)}, u32[]{:S(2)}, u32[]{:S(2)}) async-start(s32[3,32,2]{0,2,1:T(2,128)} %bitcast), calls=%async_computation | async-start | bytes 65536 | tf_op jit(solution)/shard_map/all_to_all | solution.py:177
  104.4 0.8 fusion.47
  105.8 7.0 %fusion.46 = (bf16[5,8,64,384]{3,2,1,0:T(8,128)(2,1)S(1)}, bf16[5,8,64,384]{3,2,1,0:T(8,128)(2,1)S(1)}, bf16[5,8,64,384]{3,2,1,0:T(8,128)(2,1)S(1)}, bf16[5,8,64...) fusion(bf16[7,10,64,384]{3,2,1,0:T(8,128)(2,1)S(1)} %pad_maximu, ...), kind=kLoop, calls=%fused_computation.85 | loop fusion | bytes 35389440 | tf_op jit(solution)/shard_map/slice | solution.py:43
  112.8 2.4 %fusion.52 = f32[2560,128]{1,0:T(8,128)S(1)} fusion(bf16[2560,384]{1,0:T(8,128)(2,1)} %bitcast.120, bf16[384,128]{1,0:T(8,128)(2,1)S(1)} %bitcast.126), kind=kOutput, calls=%fused_computation.91 | convolution fusion | flops 251658240 | bytes 3375104 | tf_op jit(solution)/shard_map/dot_general | solution.py:44
  115.2 0.7 convolution_add_fusion.7
  115.9 0.7 convolution_add_fusion.6
  116.6 0.7 convolution_add_fusion.5
  117.3 0.7 convolution_add_fusion.4
  118.0 0.7 convolution_add_fusion.3
  118.7 0.7 convolution_add_fusion.2
  119.4 0.7 convolution_add_fusion.1
  120.1 0.7 convolution_add_fusion
  121.0 1.5 collective-permute-start.2
  122.6 5.4 %collective-permute-done.2 = bf16[5,1,64,128]{3,2,1,0:T(8,128)(2,1)S(1)} collective-permute-done((bf16[5,1,64,128]{3,2,1,0:T(8,128)(2,1)S(1)}, bf16[5,1,64,128]{3,2,1,0:T(8,128)(2,1)S(1)}, u32[]{:S(2)}, u32[]{:S(2)}) %collective-permute-start.2) | collective-permute-done | bytes 81952 | tf_op jit(solution)/shard_map/ppermute | solution.py:32
  133.9 12.5 %all-to-all-start.1 = ((bf16[3,32,2,128]{3,2,0,1:T(2,128)(2,1)}), bf16[3,32,2,128]{3,2,0,1:T(2,128)(2,1)S(1)}, u32[]{:S(2)}, u32[]{:S(2)}) async-start(bf16[3,32,2,128]{3,2,0,1:T(2,128)(2,1)} %copy.22), calls=%async_computation.1 | async-start | bytes 98304 | tf_op jit(solution)/shard_map/all_to_all | solution.py:176
  146.5 12.4 %all-to-all-done.1 = bf16[3,32,2,128]{3,2,0,1:T(2,128)(2,1)S(1)} async-done(((bf16[3,32,2,128]{3,2,0,1:T(2,128)(2,1)}), bf16[3,32,2,128]{3,2,0,1:T(2,128)(2,1)S(1)}, u32[]{:S(2)}, u32[]{:S(2)}) %all-to-all-start.1) | async-done | bytes 49184 | tf_op jit(solution)/shard_map/all_to_all | solution.py:176
  159.0 0.8 convolution_convert_fusion
  (88 shorter events, 9.1 us)
Async XLA Ops:
  0.0 132.3 %copy-start = (bf16[128,32]{0,1:T(8,128)(2,1)S(1)}, bf16[128,32]{0,1:T(8,128)(2,1)}, u32[]{:S(2)}) copy-start(bf16[128,32]{0,1:T(8,128)(2,1)} %param.22) | copy-start | bytes 24580
  0.0 66.7 %copy-start.1 = (bf16[1,5,8,64,128]{4,3,2,1,0:T(8,128)(2,1)S(1)}, bf16[1,5,8,64,128]{4,3,2,1,0:T(8,128)(2,1)}, u32[]{:S(2)}) copy-start(bf16[1,5,8,64,128]{4,3,2,1,0:T(8,128)(2,1)} %param.13) | copy-start | bytes 1966084
  0.0 66.7 %copy-start.9 = (f32[128]{0:T(128)S(1)}, f32[128]{0:T(128)}, u32[]{:S(2)}) copy-start(f32[128]{0:T(128)} %param.14) | copy-start | bytes 1540
  0.0 66.7 %copy-start.8 = (f32[128]{0:T(128)S(1)}, f32[128]{0:T(128)}, u32[]{:S(2)}) copy-start(f32[128]{0:T(128)} %param.15) | copy-start | bytes 1540
  1.5 70.3 %copy-start.6 = (s32[1,3,32]{2,0,1:T(1,128)S(1)}, s32[1,3,32]{2,0,1:T(1,128)}, u32[]{:S(2)}) copy-start(s32[1,3,32]{2,0,1:T(1,128)} %param.24) | copy-start | bytes 1156
  36.0 36.2 %copy-start.7 = (s32[1,3,32]{2,0,1:T(1,128)S(1)}, s32[1,3,32]{2,0,1:T(1,128)}, u32[]{:S(2)}) copy-start(s32[1,3,32]{2,0,1:T(1,128)} %param.25) | copy-start | bytes 1156
  36.2 67.7 %copy-start.3 = (bf16[3,3,3,128,128]{4,3,2,1,0:T(8,128)(2,1)S(1)}, bf16[3,3,3,128,128]{4,3,2,1,0:T(8,128)(2,1)}, u32[]{:S(2)}) copy-start(bf16[3,3,3,128,128]{4,3,2,1,0:T(8,128)(2,1)} %param.16) | copy-start | bytes 2654212
  67.2 36.8 %collective-permute-start = (bf16[5,1,64,128]{3,2,1,0:T(8,128)(2,1)S(1)}, bf16[5,1,64,128]{3,2,1,0:T(8,128)(2,1)S(1)}, u32[]{:S(2)}, u32[]{:S(2)}) collective-permute-start(bf16[5,1,64,128]{3,2,1,0:T(8,128)(2,1)S(1)} %get-tuple-element.29), channel_id=1, source_target_pairs={{0,1},{1,2},{2,3},{3,4},{4,5},{5,6},{6,7},{7,8},{8,9},{9,10},{10,1... | collective-permute-start | bytes 245768 | tf_op jit(solution)/shard_map/ppermute | solution.py:20
  70.6 33.4 %collective-permute-start.1 = (bf16[5,1,64,128]{3,2,1,0:T(8,128)(2,1)S(1)}, bf16[5,1,64,128]{3,2,1,0:T(8,128)(2,1)S(1)}, u32[]{:S(2)}, u32[]{:S(2)}) collective-permute-start(bf16[5,1,64,128]{3,2,1,0:T(8,128)(2,1)S(1)} %get-tuple-element.30), channel_id=1, source_target_pairs={{1,0},{2,1},{3,2},{4,3},{5,4},{6,5},{7,6},{8,7},{9,8},{10,9},{11,1... | collective-permute-start | bytes 245768 | tf_op jit(solution)/shard_map/ppermute | solution.py:22
  73.2 60.7 %all-to-all-start = ((s32[3,32,2]{0,2,1:T(2,128)}), s32[3,32,2]{0,2,1:T(2,128)S(1)}, u32[]{:S(2)}, u32[]{:S(2)}) async-start(s32[3,32,2]{0,2,1:T(2,128)} %bitcast), calls=%async_computation | async-start | bytes 65536 | tf_op jit(solution)/shard_map/all_to_all | solution.py:177
  112.8 2.4 %copy-start.2 = (bf16[5,8,64,384]{3,2,1,0:T(8,128)(2,1)S(1)}, bf16[5,8,64,384]{3,2,1,0:T(8,128)(2,1)}, u32[]{:S(2)}) copy-start(bf16[5,8,64,384]{3,2,1,0:T(8,128)(2,1)} %get-tuple-element.12) | copy-start | bytes 5898244
  120.1 0.7 copy-start.13
  120.8 1.7 %copy-start.4 = (bf16[3,3,128,128]{3,2,1,0:T(8,128)(2,1)S(1)}, bf16[3,3,128,128]{3,2,1,0:T(8,128)(2,1)}, u32[]{:S(2)}) copy-start(bf16[3,3,128,128]{3,2,1,0:T(8,128)(2,1)} %param.18) | copy-start | bytes 884740
  121.0 6.9 %collective-permute-start.2 = (bf16[5,1,64,128]{3,2,1,0:T(8,128)(2,1)S(1)}, bf16[5,1,64,128]{3,2,1,0:T(8,128)(2,1)S(1)}, u32[]{:S(2)}, u32[]{:S(2)}) collective-permute-start(bf16[5,1,64,128]{3,2,1,0:T(8,128)(2,1)S(1)} %slice.194), channel_id=1, source_target_pairs={{1,0},{2,1},{3,2},{4,3},{5,4},{6,5},{7,6},{8,7},{9,8},{10,9},{11,1... | collective-permute-start | bytes 245768 | tf_op jit(solution)/shard_map/ppermute | solution.py:32
  130.8 0.7 copy-start.10
  131.1 0.9 copy-start.5
  131.1 1.2 copy-start.11
  131.1 1.2 copy-start.12
  133.9 25.1 %all-to-all-start.1 = ((bf16[3,32,2,128]{3,2,0,1:T(2,128)(2,1)}), bf16[3,32,2,128]{3,2,0,1:T(2,128)(2,1)S(1)}, u32[]{:S(2)}, u32[]{:S(2)}) async-start(bf16[3,32,2,128]{3,2,0,1:T(2,128)(2,1)} %copy.22), calls=%async_computation.1 | async-start | bytes 98304 | tf_op jit(solution)/shard_map/all_to_all | solution.py:176
where the time goes:
time: 160 us
  blocking collectives  62.8 us (39%)
  starting transfers between devices  49.3 us (31%)
  waiting for transfers between devices  17.9 us (11%)
  local copies, waits for them, and re-layouts  12.9 us (8%)
  matrix products  10.4 us (6%)
  other arithmetic  5.89 us (4%)
    psum x1, blocking collectives, local(): group_mean = lax.psum(local_sum, 'frame') / entries  34.3 us
    all_to_all x1, starting transfers between devices, local(): lax.all_to_all(out_slot, 'clip', split_axis=1, concat_axis=1, tiled=True)  30.7 us
    psum x1, blocking collectives, local(): lax.psum(jnp.sum(centred * centred, axis=(0, 1, 2, 4)), 'frame') / entries  28.5 us
    all_to_all x1, starting transfers between devices, local(): lax.all_to_all(outgoing, 'clip', split_axis=1, concat_axis=1, tiled=True)  12.5 us
    all_to_all x1, waiting for transfers between devices, local(): lax.all_to_all(outgoing, 'clip', split_axis=1, concat_axis=1, tiled=True)  12.4 us
    dot_general x9, matrix products, causal_mix(): jnp.dot(stacked.reshape(-1, 3 * channels), weight[time_tap, row_tap].resh...  7.85 us
    slice x1, local copies, waits for them, and re-layouts, causal_mix(): col_stack[time_tap:time_tap + frame_count, row_tap:row_tap + row_count]  7.03 us
    ppermute x1, waiting for transfers between devices, from_behind(): return lax.ppermute(block, axis, route)  5.42 us
  transfers between devices with their start and end apart: 5, of which 2 were waited for; matrix products, arithmetic and copies ran while one was open for 15% of the time, Pallas kernels for 0%

commit v1 on v0

--- a/solution.py
+++ b/solution.py
@@ -7,29 +7,6 @@
 
 
 EPSILON = 1e-06
-
-
-def with_halo(cells, sides, width):
-    for axis, dim in sides:
-        count = lax.axis_size(axis)
-        ends = count - 1
-        head = lax.slice_in_dim(cells, 0, width, axis=dim)
-        tail = lax.slice_in_dim(cells, cells.shape[dim] - width, cells.shape[dim], axis=dim)
-        cells = jnp.concatenate(
-            [
-                lax.ppermute(tail, axis, [(i, (i + 1) % count) for i in range(ends)]),
-                cells,
-                lax.ppermute(head, axis, [((i + 1) % count, i) for i in range(ends)]),
-            ],
-            axis=dim,
-        )
-    return cells
-
-
-def from_behind(block, axis, distance):
-    devices = range(lax.axis_size(axis))
-    route = [(i - distance, i) for i in devices if i - distance in devices]
-    return lax.ppermute(block, axis, route)
 
 
 def causal_mix(stacked_pad, weight, bias_vec, frame_count, row_count, col_count):
@@ -121,22 +98,35 @@
     frame_count, row_count, col_count, channels = activations.shape
     frame_devs = lax.axis_size("frame")
     position = lax.axis_index("frame")
-    entries = frame_count * frame_devs * row_count * col_count * (channels // GROUPS)
-    grouped = activations.reshape(frame_count, row_count, col_count, GROUPS, channels // GROUPS)
-    local_sum = jnp.sum(grouped, axis=(0, 1, 2, 4), dtype=jnp.float32)
-    group_mean = lax.psum(local_sum, "frame") / entries
-    centred = grouped.astype(jnp.float32) - group_mean[:, None]
-    group_var = lax.psum(jnp.sum(centred * centred, axis=(0, 1, 2, 4)), "frame") / entries
+    per_group = channels // GROUPS
+    onward = [(i, i + 1) for i in range(frame_devs - 1)]
+    back = [(i + 1, i) for i in range(frame_devs - 1)]
+    above = lax.ppermute(activations[:, row_count - 1 :], "frame", onward)
+    below = lax.ppermute(activations[:, :2], "frame", back)
+    count = frame_count * row_count * col_count
+    values = activations.astype(jnp.float32)
+    local_sum = jnp.sum(values, axis=(0, 1, 2))
+    centred = values - local_sum / count
+    local_dev = jnp.sum(centred * centred, axis=(0, 1, 2))
+    stats = jnp.broadcast_to(jnp.stack([local_sum, local_dev])[None], (frame_devs, 2, channels))
+    stats = lax.all_to_all(stats, "frame", split_axis=0, concat_axis=0, tiled=True)
+    sums = stats[:, 0].reshape(frame_devs, GROUPS, per_group)
+    devs = stats[:, 1].reshape(frame_devs, GROUPS, per_group)
+    entries = count * frame_devs * per_group
+    group_mean = jnp.sum(sums, axis=(0, 2)) / entries
+    off = sums / count - group_mean[None, :, None]
+    group_var = jnp.sum(devs + count * off * off, axis=(0, 2)) / entries
     inverse = lax.rsqrt(group_var + EPSILON)
-    hidden = normalize(activations, group_mean, inverse, norm_gain, norm_bias).astype(jnp.bfloat16)
-    hidden_ext = with_halo(hidden, (("frame", 1),), 1)
-    hidden_pad = jnp.pad(hidden_ext, ((2, 0), (0, 0), (1, 1), (0, 0)))
-    mixed = causal_mix(hidden_pad, conv_weight, conv_bias, frame_count, row_count, col_count)
-    with_skip = (activations.astype(jnp.float32) + mixed).astype(jnp.bfloat16)
-    following = from_behind(with_skip[:, :1], "frame", -1)
-    padded = jnp.pad(
-        jnp.concatenate([with_skip, following], axis=1), ((0, 0), (0, 0), (0, 1), (0, 0))
-    )
+    rows = jnp.concatenate([above, activations, below], axis=1)
+    hidden = normalize(rows, group_mean, inverse, norm_gain, norm_bias)
+    row_ids = position * row_count - 1 + jnp.arange(row_count + 3)
+    inside = (row_ids >= 0) & (row_ids < frame_devs * row_count)
+    hidden = jnp.where(inside[None, :, None, None], hidden, 0.0).astype(jnp.bfloat16)
+    hidden_pad = jnp.pad(hidden, ((2, 0), (0, 0), (1, 1), (0, 0)))
+    mixed = causal_mix(hidden_pad, conv_weight, conv_bias, frame_count, row_count + 1, col_count)
+    with_skip = rows[:, 1 : row_count + 2].astype(jnp.float32) + mixed
+    with_skip = jnp.where(inside[None, 1 : row_count + 2, None, None], with_skip, 0.0)
+    padded = jnp.pad(with_skip.astype(jnp.bfloat16), ((0, 0), (0, 0), (0, 1), (0, 0)))
     reduced = strided_mix(padded, down_weight, down_bias, row_count // 2, col_count // 2).astype(
         jnp.bfloat16
     )
@@ -146,43 +136,37 @@
     )
     latent = project_head(lat_mixed, head_weight, head_bias)
     patch_tiles = to_tiles(latent)
-    lat_count = patch_tiles.shape[0]
-    tile_count = patch_tiles.shape[1]
-    tile_width = patch_tiles.shape[2]
+    lat_count, tile_count, tile_width = patch_tiles.shape
+    shards = lax.axis_size("clip")
+    slot_block = 2 * shards
     shard_ids = tile_shard[0]
-    shards = lax.axis_size("clip")
-    pair_slots = 2 * (tile_count // shards)
-    slot_block = shards * pair_slots
     slot_ids = tile_slot[0] - position * slot_block
-    matches = (shard_ids[:, :, None] == jnp.arange(shards, dtype=jnp.int32)[None, None, :]).astype(
-        jnp.int32
+    earlier = jnp.arange(tile_count)[None, :, None] > jnp.arange(tile_count)[None, None, :]
+    same = shard_ids[:, :, None] == shard_ids[:, None, :]
+    rank_in = jnp.sum((same & earlier).astype(jnp.int32), axis=-1)
+    pair = 2 * jnp.arange(lat_count, dtype=jnp.int32)[:, None] + rank_in
+    target = (shard_ids * 8 + pair).reshape(-1)
+    tiles = patch_tiles.reshape(lat_count * tile_count, tile_width)
+    chooser = target[None, :] == jnp.arange(8 * shards, dtype=jnp.int32)[:, None]
+    outgoing = jnp.dot(
+        chooser.astype(jnp.bfloat16), tiles, preferred_element_type=jnp.float32
+    ).reshape(shards, 8, tile_width)
+    slot_of = jnp.sum(
+        jnp.where(chooser, slot_ids.reshape(-1)[None, :] + 1, 0), axis=-1
+    ).reshape(shards, 1, 8)
+    slot_row = jnp.pad(slot_of, ((0, 0), (0, 0), (0, tile_width - 8))).astype(jnp.float32)
+    is_slot = jnp.arange(8)[None, :, None] == 6
+    outgoing = jnp.where(is_slot, slot_row, outgoing).astype(jnp.bfloat16)
+    arrived = lax.all_to_all(outgoing, "clip", split_axis=0, concat_axis=0, tiled=True)
+    slots = arrived[:, 6, :8].astype(jnp.int32)
+    want = jnp.arange(lat_count * slot_block, dtype=jnp.int32)
+    have = slots - 1 + slot_block * (jnp.arange(8, dtype=jnp.int32) // 2)[None, :]
+    have = jnp.where(slots > 0, have, -1).reshape(-1)
+    placer = (want[:, None] == have[None, :]).astype(jnp.bfloat16)
+    packed = jnp.dot(
+        placer, arrived.reshape(8 * shards, tile_width), preferred_element_type=jnp.float32
     )
-    rank_in = jnp.sum((jnp.cumsum(matches, axis=1) - 1) * matches, axis=-1)
-    target = shard_ids * pair_slots + rank_in
-    chooser = target[:, None, :] == jnp.arange(slot_block, dtype=jnp.int32)[None, :, None]
-    outgoing = jnp.einsum(
-        "lpt,ltc->lpc",
-        chooser.astype(jnp.bfloat16),
-        patch_tiles,
-        preferred_element_type=jnp.float32,
-    ).astype(jnp.bfloat16)
-    filled = jnp.any(chooser, axis=-1).astype(jnp.int32)
-    out_slot = jnp.sum(jnp.where(chooser, slot_ids[:, None, :], 0), axis=-1) + slot_block * (
-        1 - filled
-    )
-    outgoing = outgoing.reshape(lat_count, shards, pair_slots, tile_width)
-    out_slot = out_slot.reshape(lat_count, shards, pair_slots)
-    arrived, arrived_slot = (
-        lax.all_to_all(outgoing, "clip", split_axis=1, concat_axis=1, tiled=True),
-        lax.all_to_all(out_slot, "clip", split_axis=1, concat_axis=1, tiled=True),
-    )
-    arrived = arrived.reshape(lat_count, slot_block, tile_width)
-    arrived_slot = arrived_slot.reshape(lat_count, slot_block)
-    placer = (
-        arrived_slot[:, None, :] == jnp.arange(slot_block, dtype=jnp.int32)[None, :, None]
-    ).astype(jnp.bfloat16)
-    packed = jnp.einsum("lqp,lpc->lqc", placer, arrived, preferred_element_type=jnp.float32)
-    return packed.astype(jnp.bfloat16)
+    return packed.reshape(lat_count, slot_block, tile_width).astype(jnp.bfloat16)
 
 
 def solution(mesh):

time: 160 us -> 85.5 us (0.53)
  the two profiles are of different devices: /device:TPU:1 before, /device:TPU:6 now
where the time goes in v1:
time: 85.5 us; the launch traced here: 85 us
  starting transfers between devices  29.7 us (35%)
  local copies, waits for them, and re-layouts  21.6 us (25%)
  waiting for transfers between devices  16.3 us (19%)
  matrix products  9.84 us (12%)
  other arithmetic  6.84 us (8%)
    all_to_all x1, waiting for transfers between devices, local(): lax.all_to_all(outgoing, 'clip', split_axis=0, concat_axis=0, tiled=True)  14.3 us
    all_to_all x1, starting transfers between devices, local(): lax.all_to_all(outgoing, 'clip', split_axis=0, concat_axis=0, tiled=True)  13.7 us
    all_to_all x1, starting transfers between devices, local(): lax.all_to_all(stats, 'frame', split_axis=0, concat_axis=0, tiled=True)  9.2 us
    dot_general x9, matrix products, causal_mix(): jnp.dot(stacked.reshape(-1, 3 * channels), weight[time_tap, row_tap].resh...  6.66 us
    slice x1, local copies, waits for them, and re-layouts, causal_mix(): col_stack[time_tap:time_tap + frame_count, row_tap:row_tap + row_count]  6.47 us
    unnamed x61, local copies, waits for them, and re-layouts  6.06 us
    ppermute x1, starting transfers between devices, local(): below = lax.ppermute(activations[:, :2], 'frame', back)  4.87 us
    ppermute x1, waiting for transfers between devices, local(): above = lax.ppermute(activations[:, row_count - 1:], 'frame', onward)  2.05 us
  transfers between devices with their start and end apart: 4, of which 2 were waited for; matrix products, arithmetic and copies ran while one was open for 7% of the time, Pallas kernels for 0%

profile of v1, /device:TPU:6, one launch (start us, length us, event | category | flops | bytes accessed | tf_op | source)
XLA Modules:
  0.0 85.0 jit_solution(8737747681895739952)
XLA Ops:
  0.0 1.5 %convert_reduce_fusion = f32[128]{0:T(128)S(1)} fusion(bf16[1,5,8,64,128]{4,3,2,1,0:T(8,128)(2,1)} %param.13), kind=kLoop, calls=%fused_computation.11 | loop fusion | flops 655232 | bytes 655872 | tf_op jit(solution)/shard_map/reduce_sum | solution.py:108
  1.6 1.5 %fusion.1 = f32[128]{0:T(128)S(1)} fusion(f32[128]{0:T(128)S(1)} %broadcast_multiply_fusion.1, bf16[1,5,8,64,128]{4,3,2,1,0:T(8,128)(2,1)} %param.13), kind=kLoop, calls=%fused_computation.17 | loop fusion | flops 1310592 | bytes 656384 | tf_op jit(solution)/shard_map/reduce_sum | solution.py:110
  3.7 9.2 %all-to-all-start = ((f32[16,2,128]{2,1,0:T(2,128)}), f32[16,2,128]{2,1,0:T(2,128)S(1)}, u32[]{:S(2)}, u32[]{:S(2)}) async-start(f32[16,2,128]{2,1,0:T(2,128)} %broadcast_in_dim.86), calls=%async_computation | async-start | bytes 32768 | tf_op jit(solution)/shard_map/all_to_all | solution.py:112
  12.9 0.9 %slice.197 = bf16[5,2,64,128]{3,2,1,0:T(8,128)(2,1)S(1)} slice(bf16[5,8,64,128]{3,2,1,0:T(8,128)(2,1)} %bitcast.89), slice={[0:5], [0:2], [0:64], [0:128]} | slice | bytes 327680 | tf_op jit(solution)/shard_map/slice | solution.py:105
  13.9 4.9 %collective-permute-start = (bf16[5,2,64,128]{3,2,1,0:T(8,128)(2,1)S(1)}, bf16[5,2,64,128]{3,2,1,0:T(8,128)(2,1)S(1)}, u32[]{:S(2)}, u32[]{:S(2)}) collective-permute-start(bf16[5,2,64,128]{3,2,1,0:T(8,128)(2,1)S(1)} %slice.197), channel_id=1, source_target_pairs={{1,0},{2,1},{3,2},{4,3},{5,4},{6,5},{7,6},{8,7},{9,8},{10,9},{11,1... | collective-permute-start | bytes 491528 | tf_op jit(solution)/shard_map/ppermute | solution.py:105
  18.7 0.9 %slice.198 = bf16[5,1,64,128]{3,2,1,0:T(8,128)(2,1)S(1)} slice(bf16[5,8,64,128]{3,2,1,0:T(8,128)(2,1)} %bitcast.90), slice={[0:5], [7:8], [0:64], [0:128]} | slice | bytes 163840 | tf_op jit(solution)/shard_map/slice | solution.py:104
  19.6 1.9 %collective-permute-start.1 = (bf16[5,1,64,128]{3,2,1,0:T(8,128)(2,1)S(1)}, bf16[5,1,64,128]{3,2,1,0:T(8,128)(2,1)S(1)}, u32[]{:S(2)}, u32[]{:S(2)}) collective-permute-start(bf16[5,1,64,128]{3,2,1,0:T(8,128)(2,1)S(1)} %slice.198), channel_id=1, source_target_pairs={{0,1},{1,2},{2,3},{3,4},{4,5},{5,6},{6,7},{7,8},{8,9},{9,10},{10,1... | collective-permute-start | bytes 245768 | tf_op jit(solution)/shard_map/ppermute | solution.py:104
  22.2 0.9 %fusion.29 = (bf16[1,1,3,128,128]{4,3,2,1,0:T(8,128)(2,1)S(1)}, bf16[1,1,3,128,128]{4,3,2,1,0:T(8,128)(2,1)}, bf16[1,1,3,128,128]{4,3,2,1,0:T(8,128)(2,1)}, bf16...) fusion(bf16[3,3,3,128,128]{4,3,2,1,0:T(8,128)(2,1)S(1)} %copy-d, ...), kind=kLoop, calls=%fused_computation.87 | loop fusion | bytes 1769472 | tf_op jit(solution)/shard_map/slice | solution.py:23
  26.0 2.1 %collective-permute-done.1 = bf16[5,1,64,128]{3,2,1,0:T(8,128)(2,1)S(1)} collective-permute-done((bf16[5,1,64,128]{3,2,1,0:T(8,128)(2,1)S(1)}, bf16[5,1,64,128]{3,2,1,0:T(8,128)(2,1)S(1)}, u32[]{:S(2)}, u32[]{:S(2)}) %collective-permute-start.1) | collective-permute-done | bytes 81952 | tf_op jit(solution)/shard_map/ppermute | solution.py:104
  28.8 1.4 %pad_slice_fusion.2 = (bf16[7,11,64,128]{3,2,1,0:T(8,128)(2,1)S(1)}, bf16[7,11,64,128]{3,2,1,0:T(8,128)(2,1)S(1)}, bf16[7,11,64,128]{3,2,1,0:T(8,128)(2,1)S(1)}) fusion(bf16[5,11,64,128]{3,2,1,0:T(8,128)(2,1)S(1)} %select_convert_fusion), kind=kLoop, calls=%fused_computation.14 | loop fusion | bytes 4685824 | tf_op jit(solution)/shard_map/slice | solution.py:15
  30.3 0.9 %pad_maximum_fusion = bf16[7,11,64,384]{3,2,1,0:T(8,128)(2,1)S(1)} fusion(bf16[7,11,64,128]{3,2,1,0:T(8,128)(2,1)S(1)} %get-tuple-element.16, bf16[7,11,64,128]{3,2,1,0:T(8,128)(2,1)S(1)} %get-tuple-element.15, bf16[7,11,64,128]{3,2,1,0:T(8,128)(2,1)S(1)} %get-tuple-element.14), kind=kLoop, calls=%fused_computation | loop fusion | flops 11354112 | bytes 7569408 | tf_op jit(solution)/shard_map/concatenate | solution.py:14
  31.2 6.5 %fusion.28 = (bf16[5,9,64,384]{3,2,1,0:T(8,128)(2,1)S(1)}, bf16[5,9,64,384]{3,2,1,0:T(8,128)(2,1)S(1)}, bf16[5,9,64,384]{3,2,1,0:T(8,128)(2,1)}, bf16[5,9,64,384...) fusion(bf16[7,11,64,384]{3,2,1,0:T(8,128)(2,1)S(1)} %pad_maximu, ...), kind=kLoop, calls=%fused_computation.86 | loop fusion | bytes 39813120 | tf_op jit(solution)/shard_map/slice | solution.py:20
  38.4 0.9 %copy-done.7 = bf16[5,9,64,384]{3,2,1,0:T(8,128)(2,1)S(1)} copy-done((bf16[5,9,64,384]{3,2,1,0:T(8,128)(2,1)S(1)}, bf16[5,9,64,384]{3,2,1,0:T(8,128)(2,1)}, u32[]{:S(2)}) %copy-start.7) | copy-done | bytes 2211864
  40.0 0.9 %copy-done.6 = bf16[5,9,64,384]{3,2,1,0:T(8,128)(2,1)S(1)} copy-done((bf16[5,9,64,384]{3,2,1,0:T(8,128)(2,1)S(1)}, bf16[5,9,64,384]{3,2,1,0:T(8,128)(2,1)}, u32[]{:S(2)}) %copy-start.6) | copy-done | bytes 2211864
  41.7 0.9 %copy-done.5 = bf16[5,9,64,384]{3,2,1,0:T(8,128)(2,1)S(1)} copy-done((bf16[5,9,64,384]{3,2,1,0:T(8,128)(2,1)S(1)}, bf16[5,9,64,384]{3,2,1,0:T(8,128)(2,1)}, u32[]{:S(2)}) %copy-start.5) | copy-done | bytes 2211864
  43.3 0.9 %copy-done.4 = bf16[5,9,64,384]{3,2,1,0:T(8,128)(2,1)S(1)} copy-done((bf16[5,9,64,384]{3,2,1,0:T(8,128)(2,1)S(1)}, bf16[5,9,64,384]{3,2,1,0:T(8,128)(2,1)}, u32[]{:S(2)}) %copy-start.4) | copy-done | bytes 2211864
  44.9 0.9 %copy-done.3 = bf16[5,9,64,384]{3,2,1,0:T(8,128)(2,1)S(1)} copy-done((bf16[5,9,64,384]{3,2,1,0:T(8,128)(2,1)S(1)}, bf16[5,9,64,384]{3,2,1,0:T(8,128)(2,1)}, u32[]{:S(2)}) %copy-start.3) | copy-done | bytes 2211864
  46.6 0.9 %copy-done.2 = bf16[5,9,64,384]{3,2,1,0:T(8,128)(2,1)S(1)} copy-done((bf16[5,9,64,384]{3,2,1,0:T(8,128)(2,1)S(1)}, bf16[5,9,64,384]{3,2,1,0:T(8,128)(2,1)}, u32[]{:S(2)}) %copy-start.2) | copy-done | bytes 2211864
  48.2 0.8 convolution_add_fusion.1
  49.0 0.8 convolution_add_fusion
  54.8 0.8 fusion.4
  55.6 13.7 %all-to-all-start.1 = ((bf16[32,8,128]{2,1,0:T(8,128)(2,1)}), bf16[32,8,128]{2,1,0:T(8,128)(2,1)S(1)}, u32[]{:S(2)}, u32[]{:S(2)}) async-start(bf16[32,8,128]{2,1,0:T(8,128)(2,1)} %fusion.4), calls=%async_computation.1 | async-start | bytes 131072 | tf_op jit(solution)/shard_map/all_to_all | solution.py:160
  69.5 14.3 %all-to-all-done.1 = bf16[32,8,128]{2,1,0:T(8,128)(2,1)S(1)} async-done(((bf16[32,8,128]{2,1,0:T(8,128)(2,1)}), bf16[32,8,128]{2,1,0:T(8,128)(2,1)S(1)}, u32[]{:S(2)}, u32[]{:S(2)}) %all-to-all-start.1) | async-done | bytes 65568 | tf_op jit(solution)/shard_map/all_to_all | solution.py:160
  84.1 0.8 convolution_convert_fusion
  (133 shorter events, 15.2 us)
Async XLA Ops:
  0.0 54.1 %copy-start = (bf16[128,32]{0,1:T(8,128)(2,1)S(1)}, bf16[128,32]{0,1:T(8,128)(2,1)}, u32[]{:S(2)}) copy-start(bf16[128,32]{0,1:T(8,128)(2,1)} %param.22) | copy-start | bytes 24580
  0.0 21.6 %copy-start.18 = (s32[1,3,32]{2,0,1:T(1,128)S(1)}, s32[1,3,32]{2,0,1:T(1,128)}, u32[]{:S(2)}) copy-start(s32[1,3,32]{2,0,1:T(1,128)} %param.24) | copy-start | bytes 1156
  0.0 22.2 %copy-start.8 = (bf16[3,3,3,128,128]{4,3,2,1,0:T(8,128)(2,1)S(1)}, bf16[3,3,3,128,128]{4,3,2,1,0:T(8,128)(2,1)}, u32[]{:S(2)}) copy-start(bf16[3,3,3,128,128]{4,3,2,1,0:T(8,128)(2,1)} %param.16) | copy-start | bytes 2654212
  0.0 23.1 %copy-start.16 = (bf16[3,3,128,128]{3,2,1,0:T(8,128)(2,1)S(1)}, bf16[3,3,128,128]{3,2,1,0:T(8,128)(2,1)}, u32[]{:S(2)}) copy-start(bf16[3,3,128,128]{3,2,1,0:T(8,128)(2,1)} %param.18) | copy-start | bytes 884740
  1.6 22.0 %copy-start.19 = (s32[1,3,32]{2,0,1:T(1,128)S(1)}, s32[1,3,32]{2,0,1:T(1,128)}, u32[]{:S(2)}) copy-start(s32[1,3,32]{2,0,1:T(1,128)} %param.25) | copy-start | bytes 1156
  1.6 26.5 %copy-start.1 = (bf16[1,5,8,64,128]{4,3,2,1,0:T(8,128)(2,1)S(1)}, bf16[1,5,8,64,128]{4,3,2,1,0:T(8,128)(2,1)}, u32[]{:S(2)}) copy-start(bf16[1,5,8,64,128]{4,3,2,1,0:T(8,128)(2,1)} %param.13) | copy-start | bytes 1966084
  1.6 26.5 %copy-start.20 = (f32[128]{0:T(128)S(1)}, f32[128]{0:T(128)}, u32[]{:S(2)}) copy-start(f32[128]{0:T(128)} %param.15) | copy-start | bytes 1540
  1.6 26.5 %copy-start.21 = (f32[128]{0:T(128)S(1)}, f32[128]{0:T(128)}, u32[]{:S(2)}) copy-start(f32[128]{0:T(128)} %param.14) | copy-start | bytes 1540
  3.7 21.4 %all-to-all-start = ((f32[16,2,128]{2,1,0:T(2,128)}), f32[16,2,128]{2,1,0:T(2,128)S(1)}, u32[]{:S(2)}, u32[]{:S(2)}) async-start(f32[16,2,128]{2,1,0:T(2,128)} %broadcast_in_dim.86), calls=%async_computation | async-start | bytes 32768 | tf_op jit(solution)/shard_map/all_to_all | solution.py:112
  13.9 14.2 %collective-permute-start = (bf16[5,2,64,128]{3,2,1,0:T(8,128)(2,1)S(1)}, bf16[5,2,64,128]{3,2,1,0:T(8,128)(2,1)S(1)}, u32[]{:S(2)}, u32[]{:S(2)}) collective-permute-start(bf16[5,2,64,128]{3,2,1,0:T(8,128)(2,1)S(1)} %slice.197), channel_id=1, source_target_pairs={{1,0},{2,1},{3,2},{4,3},{5,4},{6,5},{7,6},{8,7},{9,8},{10,9},{11,1... | collective-permute-start | bytes 491528 | tf_op jit(solution)/shard_map/ppermute | solution.py:105
  19.6 8.4 %collective-permute-start.1 = (bf16[5,1,64,128]{3,2,1,0:T(8,128)(2,1)S(1)}, bf16[5,1,64,128]{3,2,1,0:T(8,128)(2,1)S(1)}, u32[]{:S(2)}, u32[]{:S(2)}) collective-permute-start(bf16[5,1,64,128]{3,2,1,0:T(8,128)(2,1)S(1)} %slice.198), channel_id=1, source_target_pairs={{0,1},{1,2},{2,3},{3,4},{4,5},{5,6},{6,7},{7,8},{8,9},{9,10},{10,1... | collective-permute-start | bytes 245768 | tf_op jit(solution)/shard_map/ppermute | solution.py:104
  31.2 6.5 %copy-start.15 = (bf16[1,1,3,128,128]{4,3,2,1,0:T(8,128)(2,1)S(1)}, bf16[1,1,3,128,128]{4,3,2,1,0:T(8,128)(2,1)}, u32[]{:S(2)}) copy-start(bf16[1,1,3,128,128]{4,3,2,1,0:T(8,128)(2,1)} %get-tuple-element.24) | copy-start | bytes 294916
  37.7 1.6 %copy-start.7 = (bf16[5,9,64,384]{3,2,1,0:T(8,128)(2,1)S(1)}, bf16[5,9,64,384]{3,2,1,0:T(8,128)(2,1)}, u32[]{:S(2)}) copy-start(bf16[5,9,64,384]{3,2,1,0:T(8,128)(2,1)} %get-tuple-element.12) | copy-start | bytes 6635524
  39.3 1.6 %copy-start.6 = (bf16[5,9,64,384]{3,2,1,0:T(8,128)(2,1)S(1)}, bf16[5,9,64,384]{3,2,1,0:T(8,128)(2,1)}, u32[]{:S(2)}) copy-start(bf16[5,9,64,384]{3,2,1,0:T(8,128)(2,1)} %get-tuple-element.11) | copy-start | bytes 6635524
  39.3 1.6 %copy-start.13 = (bf16[1,1,3,128,128]{4,3,2,1,0:T(8,128)(2,1)S(1)}, bf16[1,1,3,128,128]{4,3,2,1,0:T(8,128)(2,1)}, u32[]{:S(2)}) copy-start(bf16[1,1,3,128,128]{4,3,2,1,0:T(8,128)(2,1)} %get-tuple-element.22) | copy-start | bytes 294916
  40.9 1.6 %copy-start.5 = (bf16[5,9,64,384]{3,2,1,0:T(8,128)(2,1)S(1)}, bf16[5,9,64,384]{3,2,1,0:T(8,128)(2,1)}, u32[]{:S(2)}) copy-start(bf16[5,9,64,384]{3,2,1,0:T(8,128)(2,1)} %get-tuple-element.10) | copy-start | bytes 6635524
  40.9 1.6 %copy-start.12 = (bf16[1,1,3,128,128]{4,3,2,1,0:T(8,128)(2,1)S(1)}, bf16[1,1,3,128,128]{4,3,2,1,0:T(8,128)(2,1)}, u32[]{:S(2)}) copy-start(bf16[1,1,3,128,128]{4,3,2,1,0:T(8,128)(2,1)} %get-tuple-element.21) | copy-start | bytes 294916
  42.6 1.6 %copy-start.4 = (bf16[5,9,64,384]{3,2,1,0:T(8,128)(2,1)S(1)}, bf16[5,9,64,384]{3,2,1,0:T(8,128)(2,1)}, u32[]{:S(2)}) copy-start(bf16[5,9,64,384]{3,2,1,0:T(8,128)(2,1)} %get-tuple-element.9) | copy-start | bytes 6635524
  42.6 1.6 %copy-start.11 = (bf16[1,1,3,128,128]{4,3,2,1,0:T(8,128)(2,1)S(1)}, bf16[1,1,3,128,128]{4,3,2,1,0:T(8,128)(2,1)}, u32[]{:S(2)}) copy-start(bf16[1,1,3,128,128]{4,3,2,1,0:T(8,128)(2,1)} %get-tuple-element.20) | copy-start | bytes 294916
  44.2 1.6 %copy-start.3 = (bf16[5,9,64,384]{3,2,1,0:T(8,128)(2,1)S(1)}, bf16[5,9,64,384]{3,2,1,0:T(8,128)(2,1)}, u32[]{:S(2)}) copy-start(bf16[5,9,64,384]{3,2,1,0:T(8,128)(2,1)} %get-tuple-element.8) | copy-start | bytes 6635524
  44.2 1.6 %copy-start.10 = (bf16[1,1,3,128,128]{4,3,2,1,0:T(8,128)(2,1)S(1)}, bf16[1,1,3,128,128]{4,3,2,1,0:T(8,128)(2,1)}, u32[]{:S(2)}) copy-start(bf16[1,1,3,128,128]{4,3,2,1,0:T(8,128)(2,1)} %get-tuple-element.19) | copy-start | bytes 294916
  45.8 1.6 %copy-start.2 = (bf16[5,9,64,384]{3,2,1,0:T(8,128)(2,1)S(1)}, bf16[5,9,64,384]{3,2,1,0:T(8,128)(2,1)}, u32[]{:S(2)}) copy-start(bf16[5,9,64,384]{3,2,1,0:T(8,128)(2,1)} %get-tuple-element.7) | copy-start | bytes 6635524
  45.8 1.6 %copy-start.9 = (bf16[1,1,3,128,128]{4,3,2,1,0:T(8,128)(2,1)S(1)}, bf16[1,1,3,128,128]{4,3,2,1,0:T(8,128)(2,1)}, u32[]{:S(2)}) copy-start(bf16[1,1,3,128,128]{4,3,2,1,0:T(8,128)(2,1)} %get-tuple-element.18) | copy-start | bytes 294916
  55.6 28.1 %all-to-all-start.1 = ((bf16[32,8,128]{2,1,0:T(8,128)(2,1)}), bf16[32,8,128]{2,1,0:T(8,128)(2,1)S(1)}, u32[]{:S(2)}, u32[]{:S(2)}) async-start(bf16[32,8,128]{2,1,0:T(8,128)(2,1)} %fusion.4), calls=%async_computation.1 | async-start | bytes 131072 | tf_op jit(solution)/shard_map/all_to_all | solution.py:160
  (10 other events, 10.4 us)

commit v2 on v1

v2 whole, which is shorter than its diff:
```python
import functools

import jax
import jax.numpy as jnp
from jax import lax
from jax.experimental import pallas as pl
from jax.experimental.pallas import tpu as pltpu
from jax.sharding import PartitionSpec as P

GROUPS = 32
EPSILON = 1e-06
PACK = 8
F32 = jnp.float32
BF16 = jnp.bfloat16


def iota(shape, dim):
    return lax.broadcasted_iota(jnp.int32, shape, dim)


def onehot(mask):
    return jnp.where(mask, 1.0, 0.0).astype(BF16)


def matmul(lhs, rhs):
    return jnp.dot(lhs, rhs, preferred_element_type=F32)


def matmul_nt(lhs, rhs):
    return lax.dot_general(lhs, rhs, (((1,), (1,)), ((), ())), preferred_element_type=F32)


def stats_kernel(x_ref, stats_ref, tail_ref, head_ref):
    frames, rows, cols, channels = x_ref.shape
    count = frames * rows * cols
    total = jnp.zeros((8, channels), F32)
    for f in range(frames):
        block = x_ref[f].astype(F32).reshape(-1, 8, channels)
        total = total + jnp.sum(block, axis=0)
    total = jnp.sum(total, axis=0, keepdims=True)
    mean = total / count
    spread = jnp.zeros((8, channels), F32)
    for f in range(frames):
        off = x_ref[f].astype(F32).reshape(-1, 8, channels) - mean
        spread = spread + jnp.sum(off * off, axis=0)
    spread = jnp.sum(spread, axis=0, keepdims=True)
    both = jnp.concatenate([total, spread], axis=0)
    for d in range(stats_ref.shape[0]):
        stats_ref[d] = both
    tail_ref[...] = x_ref[:, rows - 1 :]
    head_ref[...] = x_ref[:, :2]


def over_group(values, width):
    lane = iota(values.shape, 1)
    size = values.shape[1]
    step = 1
    while step < width:
        after = pltpu.roll(values, size - step, 1)
        before = pltpu.roll(values, step, 1)
        values = values + jnp.where((lane // step) % 2 == 0, after, before)
        step *= 2
    return values


def encode_kernel(
    pos_ref, x_ref, up_ref, dn_ref, stats_ref, vec_ref, cw_ref, dw_ref, tw_ref, hw_ref,
    shard_ref, slot_ref, out_ref, raw, hid, skip, red,
):
    frames, rows, cols, channels = x_ref.shape
    pairs = cols // 2
    devices = stats_ref.shape[0]
    per_group = channels // GROUPS
    count = frames * rows * cols
    lats = (frames + 1) // 2
    ext = rows + 3
    made = rows + 1

    stats = stats_ref[...]
    sums, devs = stats[:, 0], stats[:, 1]
    entries = count * devices * per_group
    mean = over_group(jnp.broadcast_to(jnp.sum(sums, axis=0, keepdims=True), (8, channels)), per_group)
    mean = mean[:1] / entries
    off = sums / count - mean
    var = jnp.sum(devs + count * (off * off), axis=0, keepdims=True)
    var = over_group(jnp.broadcast_to(var, (8, channels)), per_group)[:1] / entries
    scale = lax.rsqrt(var + EPSILON) * vec_ref[0:1] * 0.5
    shift = vec_ref[1:2] * 0.5

    place = pos_ref[0]
    has_up = jnp.where(place > 0, 1.0, 0.0).astype(F32)
    has_dn = jnp.where(place < devices - 1, 1.0, 0.0).astype(F32)

    def row(f, r):
        if r == 0:
            return up_ref[f, 0]
        if r <= rows:
            return x_ref[f, r - 1]
        return dn_ref[f, r - 1 - rows]

    pair_id = iota((pairs, channels), 0)
    conv_bias = vec_ref[2:3]
    for f in range(frames):
        for r in range(ext):
            raw[f, r] = row(f, r).astype(F32)
            halves = []
            for parity in range(2):
                half = (raw[f, r, pl.ds(parity, pairs, stride=2), :] - mean) * scale + shift
                half = half + half * jnp.tanh(half)
                if r == 0:
                    half = half * has_up
                elif r > rows:
                    half = half * has_dn
                halves.append(half)
            even, odd = halves
            left = jnp.where(pair_id == 0, 0.0, pltpu.roll(odd, 1, 0))
            right = jnp.where(pair_id == pairs - 1, 0.0, pltpu.roll(even, pairs - 1, 0))
            for u, part in enumerate((left, even, odd, right)):
                hid[f, r, :, u * channels : (u + 1) * channels] = part.astype(BF16)

    none = jnp.zeros((channels, channels), BF16)

    def pair_weight(a, b):
        w = [cw_ref[a, b, e] for e in range(3)]
        return jnp.concatenate(
            [
                jnp.concatenate([w[0], w[1], w[2], none], axis=0),
                jnp.concatenate([none, w[0], w[1], w[2]], axis=0),
            ],
            axis=1,
        )

    for f in range(frames):
        acc = jnp.zeros((made * pairs, 2 * channels), F32)
        for a in range(3):
            g = f - 2 + a
            if g < 0:
                continue
            for b in range(3):
                lhs = hid[g, b : b + made].reshape(made * pairs, 4 * channels)
                acc = acc + matmul(lhs, pair_weight(a, b))
        for r in range(made):
            block = acc[r * pairs : (r + 1) * pairs]
            ends = []
            for parity in range(2):
                half = block[:, parity * channels : (parity + 1) * channels] + conv_bias
                half = half + raw[f, r + 1, pl.ds(parity, pairs, stride=2), :]
                if r == rows:
                    half = half * has_dn
                ends.append(half)
            right = jnp.where(pair_id == pairs - 1, 0.0, pltpu.roll(ends[0], pairs - 1, 0))
            for u, part in enumerate((*ends, right)):
                skip[f, r, :, u * channels : (u + 1) * channels] = part.astype(BF16)

    down = jnp.concatenate([dw_ref[b, e] for b in range(3) for e in range(3)], axis=0)
    spots = rows // 2 * pairs
    for f in range(frames):
        lhs = jnp.concatenate(
            [
                jnp.concatenate([skip[f, 2 * i + b] for i in range(rows // 2)], axis=0)
                for b in range(3)
            ],
            axis=1,
        )
        red[f] = (matmul(lhs, down) + vec_ref[3:4]).astype(BF16)

    blank = jnp.zeros((spots, channels), BF16)
    taps = jnp.concatenate(
        [
            jnp.concatenate(
                [red[2 * l - 2 + k] if 2 * l - 2 + k >= 0 else blank for k in range(3)], axis=1
            )
            for l in range(lats)
        ],
        axis=0,
    )
    mixing = jnp.concatenate([tw_ref[k] for k in range(3)], axis=0)
    mixed = (matmul(taps, mixing) + vec_ref[4:5]).astype(BF16)
    width = hw_ref.shape[1]
    copies = channels // width
    spread = onehot(iota((width, channels), 1) % width == iota((width, channels), 0))
    head = matmul(hw_ref[...], spread).astype(BF16)
    latent = matmul(mixed, head) + vec_ref[5:6]
    spot = iota(latent.shape, 0) % spots
    corner = (spot // pairs) % 2 * 2 + spot % 2
    latent = jnp.where(iota(latent.shape, 1) // width == corner, latent, 0.0).astype(BF16)

    tiles = shard_ref.shape[2]
    shards = out_ref.shape[0] // PACK
    slot_base = place * (2 * shards)
    upper = onehot(iota((tiles, tiles), 0) < iota((tiles, tiles), 1))
    half_pairs = pairs // 2
    at = iota((tiles, spots), 1)
    grown = onehot(at // (2 * pairs) * half_pairs + at % pairs // 2 == iota((tiles, spots), 0))
    out = jnp.zeros(out_ref.shape, F32)
    slots = jnp.zeros((shards, channels), F32)
    for l in range(lats):
        shard = jnp.broadcast_to(shard_ref[0, l : l + 1], (shards, tiles))
        mine = shard == iota((shards, tiles), 0)
        earlier = matmul(onehot(mine), upper)
        rank = jnp.sum(jnp.where(mine, earlier, 0.0), axis=0, keepdims=True)
        key = shard_ref[0, l : l + 1].astype(F32) * PACK + 2 * l + rank
        key = matmul(jnp.broadcast_to(key, (8, tiles)).astype(BF16), grown)[:1].astype(jnp.int32)
        chosen = onehot(iota((out_ref.shape[0], spots), 0) == key)
        out = out + matmul(chosen, latent[l * spots : (l + 1) * spots])
        number = jnp.broadcast_to(slot_ref[0, l : l + 1] - slot_base + 1, (shards, tiles))
        number = jnp.where(mine, number.astype(F32), 0.0).astype(BF16)
        which = jnp.broadcast_to(rank.astype(jnp.int32) + 2 * l, (channels, tiles))
        slots = slots + matmul_nt(number, onehot(which == iota((channels, tiles), 0)))
    line = iota((out_ref.shape[0], shards), 0)
    put = onehot((line % PACK == PACK - 2) & (line // PACK == iota(line.shape, 1)))
    out_ref[...] = (out + matmul(put, slots.astype(BF16))).astype(BF16)


def place_kernel(got_ref, out_ref):
    lines, width = got_ref.shape
    slots = out_ref.shape[0]
    got = got_ref[...]
    here, there = iota((lines, lines), 0), iota((lines, lines), 1)
    table = matmul(onehot(there == here // PACK * PACK + PACK - 2), got)
    own = iota(table.shape, 0) % PACK
    table = jnp.where((iota(table.shape, 1) == own) & (own < PACK - 2), table, 0.0).astype(BF16)
    slot = matmul_nt(jnp.ones((8, width), BF16), table)[:1].astype(jnp.int32)
    line = iota((1, lines), 1)
    per_lat = slots // ((PACK - 2) // 2)
    want = jnp.where(slot > 0, slot - 1 + line % PACK // 2 * per_lat, -1)
    out_ref[...] = matmul(onehot(iota((slots, lines), 0) == want), got).astype(BF16)


def vmem(count):
    return [pl.BlockSpec(memory_space=pltpu.VMEM)] * count


def local(
    inputs,
    norm_gain,
    norm_bias,
    conv_weight,
    conv_bias,
    down_weight,
    down_bias,
    time_weight,
    time_bias,
    head_weight,
    head_bias,
    tile_shard,
    tile_slot,
):
    activations = inputs[0]
    frames, rows, cols, channels = activations.shape
    devices = lax.axis_size("frame")
    shards = lax.axis_size("clip")
    lats = (frames + 1) // 2
    position = lax.axis_index("frame").astype(jnp.int32).reshape(1)

    stats, tail, head = pl.pallas_call(
        stats_kernel,
        out_shape=(
            jax.ShapeDtypeStruct((devices, 2, channels), F32),
            jax.ShapeDtypeStruct((frames, 1, cols, channels), BF16),
            jax.ShapeDtypeStruct((frames, 2, cols, channels), BF16),
        ),
        in_specs=vmem(1),
        out_specs=tuple(vmem(3)),
        compiler_params=pltpu.CompilerParams(vmem_limit_bytes=8 << 20),
        name="stats",
    )(activations)
    stats = lax.all_to_all(stats, "frame", split_axis=0, concat_axis=0, tiled=True)
    above = lax.ppermute(tail, "frame", [(i, i + 1) for i in range(devices - 1)])
    below = lax.ppermute(head, "frame", [(i + 1, i) for i in range(devices - 1)])
    vectors = jnp.stack(
        [
            norm_gain,
            norm_bias,
            conv_bias,
            down_bias,
            time_bias,
            jnp.tile(head_bias, channels // head_bias.shape[0]),
            norm_gain,
            norm_gain,
        ]
    )
    outgoing = pl.pallas_call(
        encode_kernel,
        out_shape=jax.ShapeDtypeStruct((shards * PACK, channels), BF16),
        in_specs=[pl.BlockSpec(memory_space=pltpu.SMEM), *vmem(11)],
        out_specs=pl.BlockSpec(memory_space=pltpu.VMEM),
        scratch_shapes=[
            pltpu.VMEM((frames, rows + 3, cols, channels), F32),
            pltpu.VMEM((frames, rows + 3, cols // 2, 4 * channels), BF16),
            pltpu.VMEM((frames, rows + 1, cols // 2, 3 * channels), BF16),
            pltpu.VMEM((frames, rows // 2 * (cols // 2), channels), BF16),
        ],
        compiler_params=pltpu.CompilerParams(vmem_limit_bytes=32 << 20),
        name="encode",
    )(
        position, activations, above, below, stats, vectors, conv_weight, down_weight,
        time_weight, head_weight, tile_shard, tile_slot,
    )
    arrived = lax.all_to_all(
        outgoing.reshape(shards, PACK, channels), "clip", split_axis=0, concat_axis=0, tiled=True
    )
    packed = pl.pallas_call(
        place_kernel,
        out_shape=jax.ShapeDtypeStruct((lats * 2 * shards, channels), BF16),
        in_specs=vmem(1),
        out_specs=pl.BlockSpec(memory_space=pltpu.VMEM),
        compiler_params=pltpu.CompilerParams(vmem_limit_bytes=8 << 20),
        name="place",
    )(arrived.reshape(shards * PACK, channels))
    return packed.reshape(lats, 2 * shards, channels)


def solution(mesh):
    placed = (
        P("clip", None, "frame", None, None),
        P(),
        P(),
        P(),
        P(),
        P(),
        P(),
        P(),
        P(),
        P(),
        P(),
        P("clip", None, "frame"),
        P("clip", None, "frame"),
    )
    return jax.shard_map(
        local,
        mesh=mesh,
        in_specs=placed,
        out_specs=P(None, ("clip", "frame"), None),
        check_vma=False,
    )
```

time: 85.5 us -> 62.8 us (0.73)
  the two profiles are of different devices: /device:TPU:6 before, /device:TPU:1 now
where the time goes in v2:
time: 62.8 us; the launch traced here: 62.4 us
  blocking collectives  30.8 us (49%)
  starting transfers between devices  14.9 us (24%)
  Pallas kernels  6.92 us (11%)
  local copies, waits for them, and re-layouts  6.83 us (11%)
  waiting for transfers between devices  2.83 us (5%)
    all_to_all x1, blocking collectives, local(): lax.all_to_all(outgoing.reshape(shards, PACK, channels), 'clip', split_ax...  30.8 us
    all_to_all x1, starting transfers between devices, local(): lax.all_to_all(stats, 'frame', split_axis=0, concat_axis=0, tiled=True)  8.85 us
    unnamed x17, local copies, waits for them, and re-layouts  5.36 us
    pallas_call x1, Pallas kernels, local(): pl.pallas_call(encode_kernel, out_shape=jax.ShapeDtypeStruct((shards * PA...  4.9 us
    ppermute x1, starting transfers between devices, local(): lax.ppermute(tail, 'frame', [(i, i + 1) for i in range(devices - 1)])  4.66 us
    all_to_all x1, waiting for transfers between devices, local(): lax.all_to_all(stats, 'frame', split_axis=0, concat_axis=0, tiled=True)  2.82 us
    ppermute x1, starting transfers between devices, local(): lax.ppermute(head, 'frame', [(i + 1, i) for i in range(devices - 1)])  1.41 us
  transfers between devices with their start and end apart: 3, of which 1 were waited for; matrix products, arithmetic and copies ran while one was open for 5% of the time, Pallas kernels for 0%

profile of v2, /device:TPU:1, one launch (start us, length us, event | category | flops | bytes accessed | tf_op | source)
XLA Modules:
  0.0 62.4 jit_solution(18141756568632073831)
XLA Ops:
  0.0 1.1 %copy-done = bf16[1,5,8,64,128]{4,3,2,1,0:T(8,128)(2,1)S(1)} copy-done((bf16[1,5,8,64,128]{4,3,2,1,0:T(8,128)(2,1)S(1)}, bf16[1,5,8,64,128]{4,3,2,1,0:T(8,128)(2,1)}, u32[]{:S(2)}) %copy-start) | copy-done | bytes 655384
  1.1 0.9 %stats.1 = (f32[16,2,128]{2,1,0:T(2,128)}, bf16[5,1,64,128]{3,2,1,0:T(8,128)(2,1)S(1)}, bf16[5,2,64,128]{3,2,1,0:T(8,128)(2,1)S(1)}) custom-call(bf16[5,8,64,128]{3,2,1,0:T(8,128)(2,1)S(1)} %bitcast.10), custom_call_target="tpu_custom_call" | custom-call | tf_op jit(solution)/shard_map/stats/pallas_call | solution.py:256
  2.0 1.4 %collective-permute-start.1 = (bf16[5,2,64,128]{3,2,1,0:T(8,128)(2,1)S(1)}, bf16[5,2,64,128]{3,2,1,0:T(8,128)(2,1)S(1)}, u32[]{:S(2)}, u32[]{:S(2)}) collective-permute-start(bf16[5,2,64,128]{3,2,1,0:T(8,128)(2,1)S(1)} %get-tuple-element.9), channel_id=1, source_target_pairs={{1,0},{2,1},{3,2},{4,3},{5,4},{6,5},{7,6},{8,7},{9,8},{10,9},{11,1... | collective-permute-start | bytes 491528 | tf_op jit(solution)/shard_map/ppermute | solution.py:270
  3.4 4.7 %collective-permute-start = (bf16[5,1,64,128]{3,2,1,0:T(8,128)(2,1)S(1)}, bf16[5,1,64,128]{3,2,1,0:T(8,128)(2,1)S(1)}, u32[]{:S(2)}, u32[]{:S(2)}) collective-permute-start(bf16[5,1,64,128]{3,2,1,0:T(8,128)(2,1)S(1)} %get-tuple-element.8), channel_id=1, source_target_pairs={{0,1},{1,2},{2,3},{3,4},{4,5},{5,6},{6,7},{7,8},{8,9},{9,10},{10,1... | collective-permute-start | bytes 245768 | tf_op jit(solution)/shard_map/ppermute | solution.py:269
  8.1 8.9 %all-to-all-start = ((f32[16,2,128]{2,1,0:T(2,128)}), f32[16,2,128]{2,1,0:T(2,128)S(1)}, u32[]{:S(2)}, u32[]{:S(2)}) async-start(f32[16,2,128]{2,1,0:T(2,128)} %get-tuple-element.10), calls=%async_computation | async-start | bytes 32768 | tf_op jit(solution)/shard_map/all_to_all | solution.py:268
  17.0 0.0 copy-done.5
  17.0 0.1 copy.14.hw_ref
  17.1 0.7 %tile.2 = f32[4,32]{1,0:T(4,128)S(1)} broadcast(f32[32]{0:T(128)} %param.23), dimensions={1} | broadcast | bytes 640 | tf_op jit(solution)/shard_map/tile | solution.py:278
  17.8 0.1 stack_tile.3
  17.8 0.7 %copy.15.shard_ref = s32[1,3,32]{2,1,0:T(4,128)S(1)} copy(s32[1,3,32]{2,0,1:T(1,128)} %param.24) | data formatting | bytes 768 | tf_op args[11]
  18.5 0.7 %copy.16.slot_ref = s32[1,3,32]{2,1,0:T(4,128)S(1)} copy(s32[1,3,32]{2,0,1:T(1,128)} %param.25) | data formatting | bytes 768 | tf_op args[12]
  19.2 0.7 %copy-done.6 = f32[128]{0:T(128)S(1)} copy-done((f32[128]{0:T(128)S(1)}, f32[128]{0:T(128)}, u32[]{:S(2)}) %copy-start.6) | copy-done | bytes 536
  19.9 0.7 %stack.25.vec_ref = f32[8,128]{1,0:T(8,128)S(1)} concatenate(f32[1,128]{1,0:T(1,128)S(1)} %bitcast.14, f32[1,128]{1,0:T(1,128)} %bitcast.17, f32[1,128]{1,0:T(1,128)} %bitcast.18, f32[1,128]{1,0:T(1,128)} %bitcast.19, f32[1,128]{1,0:T(1,128)} %bitcast.20, f32[1,128]{1,0:T(1,128)S(1)} %stack_tile.3, f32[1,128]{1,0:T(1,128)S(1)} %bitcast.15, f32[1,128]{1,0:T(1,128)S(1)} %bitcast.16), dimensions={0} | concatenate | bytes 8192 | tf_op jit(solution)/shard_map/stack | solution.py:271
  20.6 2.8 %all-to-all-done.stats_ref = f32[16,2,128]{2,1,0:T(2,128)S(1)} async-done(((f32[16,2,128]{2,1,0:T(2,128)}), f32[16,2,128]{2,1,0:T(2,128)S(1)}, u32[]{:S(2)}, u32[]{:S(2)}) %all-to-all-start) | async-done | bytes 16416 | tf_op jit(solution)/shard_map/all_to_all | solution.py:268
  23.4 0.0 collective-permute-done.up_ref
  23.4 0.0 collective-permute-done.1.dn_ref
  23.4 0.0 copy-done.1
  23.4 0.0 copy-done.4
  23.4 0.0 copy-start.2
  23.4 1.2 %copy-done.2 = bf16[3,3,3,128,128]{4,3,2,1,0:T(8,128)(2,1)S(1)} copy-done((bf16[3,3,3,128,128]{4,3,2,1,0:T(8,128)(2,1)S(1)}, bf16[3,3,3,128,128]{4,3,2,1,0:T(8,128)(2,1)}, u32[]{:S(2)}) %copy-start.2) | copy-done | bytes 884760
  24.6 1.0 %copy-done.3 = bf16[3,3,128,128]{3,2,1,0:T(8,128)(2,1)S(1)} copy-done((bf16[3,3,128,128]{3,2,1,0:T(8,128)(2,1)S(1)}, bf16[3,3,128,128]{3,2,1,0:T(8,128)(2,1)}, u32[]{:S(2)}) %copy-start.3) | copy-done | bytes 294936
  25.6 4.9 %encode.1 = bf16[256,128]{1,0:T(8,128)(2,1)S(1)} custom-call(s32[1]{0:T(128)} %bitcast.pos_ref, bf16[5,8,64,128]{3,2,1,0:T(8,128)(2,1)S(1)} %bitcast.11, bf16[5,1,64,128]{3,2,1,0:T(8,128)(2,1)S(1)} %collective-permute-done.up_ref, bf16[5,2,64,128]{3,2,1,0:T(8,128)(2,1)S(1)} %collective-permute-done.1.dn_ref, f32[16,2,128]{2,1,0:T(2,128)S(1)} %all-to-all-done.stats_ref, ...), custom_call_target="tpu_custom_call" | custom-call | tf_op jit(solution)/shard_map/encode/pallas_call | solution.py:283
  30.5 30.8 %all_to_all.10 = bf16[32,8,128]{2,1,0:T(8,128)(2,1)S(1)} all-to-all(bf16[32,8,128]{2,1,0:T(8,128)(2,1)S(1)} %bitcast.12), channel_id=1, replica_groups=mesh['clip'=32,'frame'=16] {'clip'}, dimensions={0} | all-to-all | bytes 131072 | tf_op jit(solution)/shard_map/all_to_all | solution.py:300
  61.3 1.1 %place.1 = bf16[192,128]{1,0:T(8,128)(2,1)} custom-call(bf16[256,128]{1,0:T(8,128)(2,1)S(1)} %bitcast.13), custom_call_target="tpu_custom_call" | custom-call | tf_op jit(solution)/shard_map/place/pallas_call | solution.py:303
  (6 shorter events, 0.0 us)
Async XLA Ops:
  0.0 1.1 %copy-start = (bf16[1,5,8,64,128]{4,3,2,1,0:T(8,128)(2,1)S(1)}, bf16[1,5,8,64,128]{4,3,2,1,0:T(8,128)(2,1)}, u32[]{:S(2)}) copy-start(bf16[1,5,8,64,128]{4,3,2,1,0:T(8,128)(2,1)} %param.13) | copy-start | bytes 1966084
  1.1 15.9 %copy-start.5 = (bf16[128,32]{0,1:T(8,128)(2,1)S(1)}, bf16[128,32]{0,1:T(8,128)(2,1)}, u32[]{:S(2)}) copy-start(bf16[128,32]{0,1:T(8,128)(2,1)} %param.22) | copy-start | bytes 24580
  1.1 22.3 %copy-start.1 = (bf16[1,5,8,64,128]{4,3,2,1,0:T(8,128)(2,1)S(1)}, bf16[1,5,8,64,128]{4,3,2,1,0:T(8,128)(2,1)}, u32[]{:S(2)}) copy-start(bf16[1,5,8,64,128]{4,3,2,1,0:T(8,128)(2,1)} %param.13) | copy-start | bytes 1966084
  2.0 21.4 %copy-start.4 = (bf16[3,128,128]{2,1,0:T(8,128)(2,1)S(1)}, bf16[3,128,128]{2,1,0:T(8,128)(2,1)}, u32[]{:S(2)}) copy-start(bf16[3,128,128]{2,1,0:T(8,128)(2,1)} %tw_ref.1) | copy-start | bytes 294916
  2.0 21.4 %collective-permute-start.1 = (bf16[5,2,64,128]{3,2,1,0:T(8,128)(2,1)S(1)}, bf16[5,2,64,128]{3,2,1,0:T(8,128)(2,1)S(1)}, u32[]{:S(2)}, u32[]{:S(2)}) collective-permute-start(bf16[5,2,64,128]{3,2,1,0:T(8,128)(2,1)S(1)} %get-tuple-element.9), channel_id=1, source_target_pairs={{1,0},{2,1},{3,2},{4,3},{5,4},{6,5},{7,6},{8,7},{9,8},{10,9},{11,1... | collective-permute-start | bytes 491528 | tf_op jit(solution)/shard_map/ppermute | solution.py:270
  3.4 20.0 %collective-permute-start = (bf16[5,1,64,128]{3,2,1,0:T(8,128)(2,1)S(1)}, bf16[5,1,64,128]{3,2,1,0:T(8,128)(2,1)S(1)}, u32[]{:S(2)}, u32[]{:S(2)}) collective-permute-start(bf16[5,1,64,128]{3,2,1,0:T(8,128)(2,1)S(1)} %get-tuple-element.8), channel_id=1, source_target_pairs={{0,1},{1,2},{2,3},{3,4},{4,5},{5,6},{6,7},{7,8},{8,9},{9,10},{10,1... | collective-permute-start | bytes 245768 | tf_op jit(solution)/shard_map/ppermute | solution.py:269
  8.1 15.3 %all-to-all-start = ((f32[16,2,128]{2,1,0:T(2,128)}), f32[16,2,128]{2,1,0:T(2,128)S(1)}, u32[]{:S(2)}, u32[]{:S(2)}) async-start(f32[16,2,128]{2,1,0:T(2,128)} %get-tuple-element.10), calls=%async_computation | async-start | bytes 32768 | tf_op jit(solution)/shard_map/all_to_all | solution.py:268
  19.2 0.7 %copy-start.6 = (f32[128]{0:T(128)S(1)}, f32[128]{0:T(128)}, u32[]{:S(2)}) copy-start(f32[128]{0:T(128)} %param.14) | copy-start | bytes 1540
  23.4 1.2 %copy-start.2 = (bf16[3,3,3,128,128]{4,3,2,1,0:T(8,128)(2,1)S(1)}, bf16[3,3,3,128,128]{4,3,2,1,0:T(8,128)(2,1)}, u32[]{:S(2)}) copy-start(bf16[3,3,3,128,128]{4,3,2,1,0:T(8,128)(2,1)} %cw_ref.1) | copy-start | bytes 2654212
  24.6 1.0 %copy-start.3 = (bf16[3,3,128,128]{3,2,1,0:T(8,128)(2,1)S(1)}, bf16[3,3,128,128]{3,2,1,0:T(8,128)(2,1)}, u32[]{:S(2)}) copy-start(bf16[3,3,128,128]{3,2,1,0:T(8,128)(2,1)} %dw_ref.1) | copy-start | bytes 884740

commit v3 on v2

--- a/solution.py
+++ b/solution.py
@@ -33,17 +33,14 @@
 def stats_kernel(x_ref, stats_ref, tail_ref, head_ref):
     frames, rows, cols, channels = x_ref.shape
     count = frames * rows * cols
-    total = jnp.zeros((8, channels), F32)
-    for f in range(frames):
-        block = x_ref[f].astype(F32).reshape(-1, 8, channels)
-        total = total + jnp.sum(block, axis=0)
-    total = jnp.sum(total, axis=0, keepdims=True)
+
+    def over_all(change):
+        parts = [jnp.sum(change(x_ref[f].astype(F32)), axis=0) for f in range(frames)]
+        return jnp.sum(sum(parts), axis=0, keepdims=True)
+
+    total = over_all(lambda v: v)
     mean = total / count
-    spread = jnp.zeros((8, channels), F32)
-    for f in range(frames):
-        off = x_ref[f].astype(F32).reshape(-1, 8, channels) - mean
-        spread = spread + jnp.sum(off * off, axis=0)
-    spread = jnp.sum(spread, axis=0, keepdims=True)
+    spread = over_all(lambda v: (v - mean) * (v - mean))
     both = jnp.concatenate([total, spread], axis=0)
     for d in range(stats_ref.shape[0]):
         stats_ref[d] = both
@@ -64,8 +61,8 @@
 
 
 def encode_kernel(
-    pos_ref, x_ref, up_ref, dn_ref, stats_ref, vec_ref, cw_ref, dw_ref, tw_ref, hw_ref,
-    shard_ref, slot_ref, out_ref, raw, hid, skip, red,
+    pos_ref, x_ref, up_ref, dn_ref, stats_ref, vec_ref, head_ref, keys_ref, slots_ref, cw_ref,
+    dw_ref, tw_ref, out_ref, raw, hid, skip, red,
 ):
     frames, rows, cols, channels = x_ref.shape
     pairs = cols // 2
@@ -176,54 +173,75 @@
     )
     mixing = jnp.concatenate([tw_ref[k] for k in range(3)], axis=0)
     mixed = (matmul(taps, mixing) + vec_ref[4:5]).astype(BF16)
-    width = hw_ref.shape[1]
-    copies = channels // width
-    spread = onehot(iota((width, channels), 1) % width == iota((width, channels), 0))
-    head = matmul(hw_ref[...], spread).astype(BF16)
-    latent = matmul(mixed, head) + vec_ref[5:6]
+    width = channels // 4
+    latent = matmul_nt(mixed, head_ref[...]) + vec_ref[5:6]
     spot = iota(latent.shape, 0) % spots
     corner = (spot // pairs) % 2 * 2 + spot % 2
     latent = jnp.where(iota(latent.shape, 1) // width == corner, latent, 0.0).astype(BF16)
 
-    tiles = shard_ref.shape[2]
-    shards = out_ref.shape[0] // PACK
-    slot_base = place * (2 * shards)
+    line = iota((out_ref.shape[0], spots), 0)
+    out = put_slots(slots_ref[...], out_ref.shape[0])
+    for l in range(lats):
+        chosen = onehot(line == keys_ref[l : l + 1])
+        out = out + matmul(chosen, latent[l * spots : (l + 1) * spots])
+    out_ref[...] = out.astype(BF16)
+
+
+def put_slots(slots, lines):
+    line = iota((lines, slots.shape[0]), 0)
+    put = onehot((line % PACK == PACK - 2) & (line // PACK == iota(line.shape, 1)))
+    return matmul(put, slots)
+
+
+def prep_kernel(*refs, pairs):
+    pos_ref, shard_ref, slot_ref, *line_refs, hw_ref = refs[:-4]
+    keys_ref, slots_ref, vec_ref, head_ref = refs[-4:]
+    copies = vec_ref.shape[1] // hw_ref.shape[0]
+    for i, ref in enumerate(line_refs):
+        row = ref[...]
+        if row.shape[1] < vec_ref.shape[1]:
+            row = jnp.concatenate([row] * copies, axis=1)
+        vec_ref[i : i + 1] = row
+    vec_ref[len(line_refs) :] = jnp.zeros((8 - len(line_refs), vec_ref.shape[1]), F32)
+    head_ref[...] = jnp.concatenate([hw_ref[...]] * copies, axis=0)
+    lats, _, tiles = shard_ref.shape
+    shards, channels = slots_ref.shape
+    spots = keys_ref.shape[1]
+    slot_base = pos_ref[0] * (2 * shards)
     upper = onehot(iota((tiles, tiles), 0) < iota((tiles, tiles), 1))
-    half_pairs = pairs // 2
     at = iota((tiles, spots), 1)
-    grown = onehot(at // (2 * pairs) * half_pairs + at % pairs // 2 == iota((tiles, spots), 0))
-    out = jnp.zeros(out_ref.shape, F32)
+    grown = at // (2 * pairs) * (pairs // 2) + at % pairs // 2
+    grown = onehot(grown == iota((tiles, spots), 0))
     slots = jnp.zeros((shards, channels), F32)
+    keys = []
     for l in range(lats):
-        shard = jnp.broadcast_to(shard_ref[0, l : l + 1], (shards, tiles))
+        shard = jnp.broadcast_to(shard_ref[l], (shards, tiles))
         mine = shard == iota((shards, tiles), 0)
         earlier = matmul(onehot(mine), upper)
         rank = jnp.sum(jnp.where(mine, earlier, 0.0), axis=0, keepdims=True)
-        key = shard_ref[0, l : l + 1].astype(F32) * PACK + 2 * l + rank
-        key = matmul(jnp.broadcast_to(key, (8, tiles)).astype(BF16), grown)[:1].astype(jnp.int32)
-        chosen = onehot(iota((out_ref.shape[0], spots), 0) == key)
-        out = out + matmul(chosen, latent[l * spots : (l + 1) * spots])
-        number = jnp.broadcast_to(slot_ref[0, l : l + 1] - slot_base + 1, (shards, tiles))
+        keys.append(shard_ref[l].astype(F32) * PACK + 2 * l + rank)
+        number = jnp.broadcast_to(slot_ref[l] - slot_base + 1, (shards, tiles))
         number = jnp.where(mine, number.astype(F32), 0.0).astype(BF16)
         which = jnp.broadcast_to(rank.astype(jnp.int32) + 2 * l, (channels, tiles))
-        slots = slots + matmul_nt(number, onehot(which == iota((channels, tiles), 0)))
-    line = iota((out_ref.shape[0], shards), 0)
-    put = onehot((line % PACK == PACK - 2) & (line // PACK == iota(line.shape, 1)))
-    out_ref[...] = (out + matmul(put, slots.astype(BF16))).astype(BF16)
+        slots = slots + matmul_nt(number, onehot(which == iota((channels, tiles), 0) % PACK))
+    keys = jnp.concatenate(keys + [jnp.zeros((8 - lats, tiles), F32)], axis=0)
+    keys_ref[...] = matmul(keys.astype(BF16), grown).astype(jnp.int32)
+    slots_ref[...] = slots.astype(BF16)
 
 
 def place_kernel(got_ref, out_ref):
     lines, width = got_ref.shape
     slots = out_ref.shape[0]
+    shards = lines // PACK
     got = got_ref[...]
-    here, there = iota((lines, lines), 0), iota((lines, lines), 1)
-    table = matmul(onehot(there == here // PACK * PACK + PACK - 2), got)
-    own = iota(table.shape, 0) % PACK
-    table = jnp.where((iota(table.shape, 1) == own) & (own < PACK - 2), table, 0.0).astype(BF16)
-    slot = matmul_nt(jnp.ones((8, width), BF16), table)[:1].astype(jnp.int32)
-    line = iota((1, lines), 1)
+    pick = iota((shards, lines), 1) == iota((shards, lines), 0) * PACK + PACK - 2
+    table = matmul(onehot(pick), got)
+    table = jnp.concatenate([table] * (lines // width), axis=1)
+    table = jnp.where(iota(table.shape, 1) // PACK == iota(table.shape, 0), table, 0.0)
+    slot = jnp.sum(table, axis=0, keepdims=True).astype(jnp.int32)
+    own = iota((1, lines), 1) % PACK
     per_lat = slots // ((PACK - 2) // 2)
-    want = jnp.where(slot > 0, slot - 1 + line % PACK // 2 * per_lat, -1)
+    want = jnp.where((slot > 0) & (own < PACK - 2), slot - 1 + own // 2 * per_lat, -1)
     out_ref[...] = matmul(onehot(iota((slots, lines), 0) == want), got).astype(BF16)
 
 
@@ -268,22 +286,33 @@
     stats = lax.all_to_all(stats, "frame", split_axis=0, concat_axis=0, tiled=True)
     above = lax.ppermute(tail, "frame", [(i, i + 1) for i in range(devices - 1)])
     below = lax.ppermute(head, "frame", [(i + 1, i) for i in range(devices - 1)])
-    vectors = jnp.stack(
-        [
-            norm_gain,
-            norm_bias,
-            conv_bias,
-            down_bias,
-            time_bias,
-            jnp.tile(head_bias, channels // head_bias.shape[0]),
-            norm_gain,
-            norm_gain,
-        ]
-    )
+    lines = [
+        v.reshape(1, -1)
+        for v in (norm_gain, norm_bias, conv_bias, down_bias, time_bias, head_bias)
+    ]
+    pairs = cols // 2
+    prepared = pl.pallas_call(
+        functools.partial(prep_kernel, pairs=pairs),
+        out_shape=(
+            jax.ShapeDtypeStruct((8, rows // 2 * pairs), jnp.int32),
+            jax.ShapeDtypeStruct((shards, channels), BF16),
+            jax.ShapeDtypeStruct((8, channels), F32),
+            jax.ShapeDtypeStruct((channels, channels), BF16),
+        ),
+        in_specs=[pl.BlockSpec(memory_space=pltpu.SMEM), *vmem(9)],
+        out_specs=tuple(vmem(4)),
+        compiler_params=pltpu.CompilerParams(vmem_limit_bytes=4 << 20),
+        cost_estimate=pl.CostEstimate(flops=20_000_000_000, bytes_accessed=0, transcendentals=0),
+        name="prep",
+    )(position, tile_shard.transpose(1, 0, 2), tile_slot.transpose(1, 0, 2), *lines, head_weight.T)
+    weights = (conv_weight, down_weight, time_weight)
     outgoing = pl.pallas_call(
         encode_kernel,
         out_shape=jax.ShapeDtypeStruct((shards * PACK, channels), BF16),
-        in_specs=[pl.BlockSpec(memory_space=pltpu.SMEM), *vmem(11)],
+        in_specs=[
+            pl.BlockSpec(memory_space=pltpu.SMEM),
+            *vmem(11),
+        ],
         out_specs=pl.BlockSpec(memory_space=pltpu.VMEM),
         scratch_shapes=[
             pltpu.VMEM((frames, rows + 3, cols, channels), F32),
@@ -294,8 +323,7 @@
         compiler_params=pltpu.CompilerParams(vmem_limit_bytes=32 << 20),
         name="encode",
     )(
-        position, activations, above, below, stats, vectors, conv_weight, down_weight,
-        time_weight, head_weight, tile_shard, tile_slot,
+        position, activations, above, below, stats, prepared[2], prepared[3], *prepared[:2], *weights
     )
     arrived = lax.all_to_all(
         outgoing.reshape(shards, PACK, channels), "clip", split_axis=0, concat_axis=0, tiled=True

time: 62.8 us -> 58 us (0.924)
  local copies, waits for them, and re-layouts: 6.83 us -> 1.83 us
  waiting for transfers between devices: 2.83 us -> 5.18 us
  starting transfers between devices: 14.9 us -> 12.9 us
    unnamed x17 -> x28, local copies, waits for them, and re-layouts: 5.36 us -> 1.83 us
    all_to_all x1, waiting for transfers between devices: 2.82 us -> 5.18 us  [local(): lax.all_to_all(stats, 'frame', split_axis=0, concat_axis=0, tiled=True)]
    another operation x3 -> x0, local copies, waits for them, and re-layouts: 1.47 us -> none  [the longest x2 0.81 us: local(): jnp.stack([norm_gain, norm_bias, conv_bias, down_bias, time_bias, jnp.til...]
    all_to_all x1, starting transfers between devices: 8.85 us -> 7.55 us  [local(): lax.all_to_all(stats, 'frame', split_axis=0, concat_axis=0, tiled=True)]
    ppermute x1, starting transfers between devices: 4.66 us -> 4.02 us  [local(): lax.ppermute(tail, 'frame', [(i, i + 1) for i in range(devices - 1)])]
  transfers between devices with their start and end apart: 3 -> 3, of which waited for: 1 -> 1; matrix products, arithmetic and copies ran while one was open for 5% -> 0% of each run, Pallas kernels for 0% -> 1%
where the time goes in v3:
time: 58 us; the launch traced here: 57.7 us
  blocking collectives  30.8 us (53%)
  starting transfers between devices  12.9 us (22%)
  Pallas kernels  6.88 us (12%)
  waiting for transfers between devices  5.18 us (9%)
  local copies, waits for them, and re-layouts  1.83 us (3%)
    all_to_all x1, blocking collectives, local(): lax.all_to_all(outgoing.reshape(shards, PACK, channels), 'clip', split_ax...  30.8 us
    all_to_all x1, starting transfers between devices, local(): lax.all_to_all(stats, 'frame', split_axis=0, concat_axis=0, tiled=True)  7.55 us
    all_to_all x1, waiting for transfers between devices, local(): lax.all_to_all(stats, 'frame', split_axis=0, concat_axis=0, tiled=True)  5.18 us
    pallas_call x1, Pallas kernels, local(): pl.pallas_call(encode_kernel, out_shape=jax.ShapeDtypeStruct((shards * PA...  4.57 us
    ppermute x1, starting transfers between devices, local(): lax.ppermute(tail, 'frame', [(i, i + 1) for i in range(devices - 1)])  4.02 us
    unnamed x28, local copies, waits for them, and re-layouts  1.83 us
    ppermute x1, starting transfers between devices, local(): lax.ppermute(head, 'frame', [(i + 1, i) for i in range(devices - 1)])  1.29 us
  transfers between devices with their start and end apart: 3, of which 1 were waited for; matrix products, arithmetic and copies ran while one was open for 0% of the time, Pallas kernels for 1%

profile of v3, /device:TPU:1, one launch (start us, length us, event | category | flops | bytes accessed | tf_op | source)
XLA Modules:
  0.0 57.7 jit_solution(5140737764317496616)
XLA Ops:
  0.0 1.1 %copy-done = bf16[1,5,8,64,128]{4,3,2,1,0:T(8,128)(2,1)S(1)} copy-done((bf16[1,5,8,64,128]{4,3,2,1,0:T(8,128)(2,1)S(1)}, bf16[1,5,8,64,128]{4,3,2,1,0:T(8,128)(2,1)}, u32[]{:S(2)}) %copy-start) | copy-done | bytes 655384
  1.1 0.9 %stats.1 = (f32[16,2,128]{2,1,0:T(2,128)}, bf16[5,1,64,128]{3,2,1,0:T(8,128)(2,1)S(1)}, bf16[5,2,64,128]{3,2,1,0:T(8,128)(2,1)S(1)}) custom-call(bf16[5,8,64,128]{3,2,1,0:T(8,128)(2,1)S(1)} %bitcast.14), custom_call_target="tpu_custom_call" | custom-call | tf_op jit(solution)/shard_map/stats/pallas_call | solution.py:274
  2.0 4.0 %collective-permute-start = (bf16[5,1,64,128]{3,2,1,0:T(8,128)(2,1)S(1)}, bf16[5,1,64,128]{3,2,1,0:T(8,128)(2,1)S(1)}, u32[]{:S(2)}, u32[]{:S(2)}) collective-permute-start(bf16[5,1,64,128]{3,2,1,0:T(8,128)(2,1)S(1)} %get-tuple-element.12), channel_id=1, source_target_pairs={{0,1},{1,2},{2,3},{3,4},{4,5},{5,6},{6,7},{7,8},{8,9},{9,10},{10,1... | collective-permute-start | bytes 245768 | tf_op jit(solution)/shard_map/ppermute | solution.py:287
  6.1 1.3 %collective-permute-start.1 = (bf16[5,2,64,128]{3,2,1,0:T(8,128)(2,1)S(1)}, bf16[5,2,64,128]{3,2,1,0:T(8,128)(2,1)S(1)}, u32[]{:S(2)}, u32[]{:S(2)}) collective-permute-start(bf16[5,2,64,128]{3,2,1,0:T(8,128)(2,1)S(1)} %get-tuple-element.13), channel_id=1, source_target_pairs={{1,0},{2,1},{3,2},{4,3},{5,4},{6,5},{7,6},{8,7},{9,8},{10,9},{11,1... | collective-permute-start | bytes 491528 | tf_op jit(solution)/shard_map/ppermute | solution.py:288
  7.4 7.6 %all-to-all-start = ((f32[16,2,128]{2,1,0:T(2,128)}), f32[16,2,128]{2,1,0:T(2,128)S(1)}, u32[]{:S(2)}, u32[]{:S(2)}) async-start(f32[16,2,128]{2,1,0:T(2,128)} %get-tuple-element.14), calls=%async_computation | async-start | bytes 32768 | tf_op jit(solution)/shard_map/all_to_all | solution.py:286
  14.9 0.0 copy-start.5
  14.9 0.0 copy-start.9
  14.9 0.0 copy-start.10
  15.0 0.0 copy-start.11
  15.0 0.0 copy-start.12
  15.0 0.0 copy-start.13
  15.0 0.0 copy-start.6
  15.0 0.0 copy-start.7
  15.0 0.0 copy-start.8
  15.0 0.6 %copy-done.5 = bf16[128,32]{0,1:T(8,128)(2,1)S(1)} copy-done((bf16[128,32]{0,1:T(8,128)(2,1)S(1)}, bf16[128,32]{0,1:T(8,128)(2,1)}, u32[]{:S(2)}) %copy-start.5) | copy-done | bytes 8216
  15.6 0.0 copy-done.12
  15.6 0.0 copy-done.13
  15.7 0.0 copy-done.6
  15.7 0.0 copy-done.7
  15.7 0.4 prep.1
  16.2 5.2 %all-to-all-done.stats_ref = f32[16,2,128]{2,1,0:T(2,128)S(1)} async-done(((f32[16,2,128]{2,1,0:T(2,128)}), f32[16,2,128]{2,1,0:T(2,128)S(1)}, u32[]{:S(2)}, u32[]{:S(2)}) %all-to-all-start) | async-done | bytes 16416 | tf_op jit(solution)/shard_map/all_to_all | solution.py:286
  21.4 4.6 %encode.1 = bf16[256,128]{1,0:T(8,128)(2,1)S(1)} custom-call(s32[1]{0:T(128)} %bitcast.refs_0_.pos_ref, bf16[5,8,64,128]{3,2,1,0:T(8,128)(2,1)S(1)} %bitcast.15, bf16[5,1,64,128]{3,2,1,0:T(8,128)(2,1)S(1)} %collective-permute-done.up_ref, bf16[5,2,64,128]{3,2,1,0:T(8,128)(2,1)S(1)} %collective-permute-done.1.dn_ref, ...), custom_call_target="tpu_custom_call" | custom-call | tf_op jit(solution)/shard_map/encode/pallas_call | solution.py:309
  26.0 30.8 %all_to_all.10 = bf16[32,8,128]{2,1,0:T(8,128)(2,1)S(1)} all-to-all(bf16[32,8,128]{2,1,0:T(8,128)(2,1)S(1)} %bitcast.16), channel_id=1, replica_groups=mesh['clip'=32,'frame'=16] {'clip'}, dimensions={0} | all-to-all | bytes 131072 | tf_op jit(solution)/shard_map/all_to_all | solution.py:328
  56.8 0.9 %place.1 = bf16[192,128]{1,0:T(8,128)(2,1)} custom-call(bf16[256,128]{1,0:T(8,128)(2,1)S(1)} %bitcast.17), custom_call_target="tpu_custom_call" | custom-call | tf_op jit(solution)/shard_map/place/pallas_call | solution.py:331
  (15 shorter events, 0.0 us)
Async XLA Ops:
  0.0 1.1 %copy-start = (bf16[1,5,8,64,128]{4,3,2,1,0:T(8,128)(2,1)S(1)}, bf16[1,5,8,64,128]{4,3,2,1,0:T(8,128)(2,1)}, u32[]{:S(2)}) copy-start(bf16[1,5,8,64,128]{4,3,2,1,0:T(8,128)(2,1)} %param.13) | copy-start | bytes 1966084
  2.0 19.3 %collective-permute-start = (bf16[5,1,64,128]{3,2,1,0:T(8,128)(2,1)S(1)}, bf16[5,1,64,128]{3,2,1,0:T(8,128)(2,1)S(1)}, u32[]{:S(2)}, u32[]{:S(2)}) collective-permute-start(bf16[5,1,64,128]{3,2,1,0:T(8,128)(2,1)S(1)} %get-tuple-element.12), channel_id=1, source_target_pairs={{0,1},{1,2},{2,3},{3,4},{4,5},{5,6},{6,7},{7,8},{8,9},{9,10},{10,1... | collective-permute-start | bytes 245768 | tf_op jit(solution)/shard_map/ppermute | solution.py:287
  6.1 15.3 %collective-permute-start.1 = (bf16[5,2,64,128]{3,2,1,0:T(8,128)(2,1)S(1)}, bf16[5,2,64,128]{3,2,1,0:T(8,128)(2,1)S(1)}, u32[]{:S(2)}, u32[]{:S(2)}) collective-permute-start(bf16[5,2,64,128]{3,2,1,0:T(8,128)(2,1)S(1)} %get-tuple-element.13), channel_id=1, source_target_pairs={{1,0},{2,1},{3,2},{4,3},{5,4},{6,5},{7,6},{8,7},{9,8},{10,9},{11,1... | collective-permute-start | bytes 491528 | tf_op jit(solution)/shard_map/ppermute | solution.py:288
  7.4 14.0 %all-to-all-start = ((f32[16,2,128]{2,1,0:T(2,128)}), f32[16,2,128]{2,1,0:T(2,128)S(1)}, u32[]{:S(2)}, u32[]{:S(2)}) async-start(f32[16,2,128]{2,1,0:T(2,128)} %get-tuple-element.14), calls=%async_computation | async-start | bytes 32768 | tf_op jit(solution)/shard_map/all_to_all | solution.py:286
  14.9 0.7 %copy-start.5 = (bf16[128,32]{0,1:T(8,128)(2,1)S(1)}, bf16[128,32]{0,1:T(8,128)(2,1)}, u32[]{:S(2)}) copy-start(bf16[128,32]{0,1:T(8,128)(2,1)} %param.22) | copy-start | bytes 24580
  14.9 0.7 %copy-start.9 = (f32[128]{0:T(128)S(1)}, f32[128]{0:T(128)}, u32[]{:S(2)}) copy-start(f32[128]{0:T(128)} %param.15) | copy-start | bytes 1540
  14.9 0.7 %copy-start.10 = (f32[128]{0:T(128)S(1)}, f32[128]{0:T(128)}, u32[]{:S(2)}) copy-start(f32[128]{0:T(128)} %param.17) | copy-start | bytes 1540
  15.0 0.7 %copy-start.11 = (f32[128]{0:T(128)S(1)}, f32[128]{0:T(128)}, u32[]{:S(2)}) copy-start(f32[128]{0:T(128)} %param.19) | copy-start | bytes 1540
  15.0 0.7 %copy-start.12 = (f32[128]{0:T(128)S(1)}, f32[128]{0:T(128)}, u32[]{:S(2)}) copy-start(f32[128]{0:T(128)} %param.21) | copy-start | bytes 1540
  15.0 0.7 %copy-start.13 = (f32[32]{0:T(128)S(1)}, f32[32]{0:T(128)}, u32[]{:S(2)}) copy-start(f32[32]{0:T(128)} %param.23) | copy-start | bytes 388
  15.0 0.7 %copy-start.6 = (s32[1,3,32]{2,0,1:T(1,128)S(1)}, s32[1,3,32]{2,0,1:T(1,128)}, u32[]{:S(2)}) copy-start(s32[1,3,32]{2,0,1:T(1,128)} %param.24) | copy-start | bytes 1156
  15.0 0.7 %copy-start.7 = (s32[1,3,32]{2,0,1:T(1,128)S(1)}, s32[1,3,32]{2,0,1:T(1,128)}, u32[]{:S(2)}) copy-start(s32[1,3,32]{2,0,1:T(1,128)} %param.25) | copy-start | bytes 1156
  15.0 0.7 %copy-start.8 = (f32[128]{0:T(128)S(1)}, f32[128]{0:T(128)}, u32[]{:S(2)}) copy-start(f32[128]{0:T(128)} %param.14) | copy-start | bytes 1540
  15.7 5.7 %copy-start.1 = (bf16[1,5,8,64,128]{4,3,2,1,0:T(8,128)(2,1)S(1)}, bf16[1,5,8,64,128]{4,3,2,1,0:T(8,128)(2,1)}, u32[]{:S(2)}) copy-start(bf16[1,5,8,64,128]{4,3,2,1,0:T(8,128)(2,1)} %param.13) | copy-start | bytes 1966084
  15.7 5.7 %copy-start.2 = (bf16[3,3,3,128,128]{4,3,2,1,0:T(8,128)(2,1)S(1)}, bf16[3,3,3,128,128]{4,3,2,1,0:T(8,128)(2,1)}, u32[]{:S(2)}) copy-start(bf16[3,3,3,128,128]{4,3,2,1,0:T(8,128)(2,1)} %cw_ref.1) | copy-start | bytes 2654212
  15.7 5.7 %copy-start.3 = (bf16[3,3,128,128]{3,2,1,0:T(8,128)(2,1)S(1)}, bf16[3,3,128,128]{3,2,1,0:T(8,128)(2,1)}, u32[]{:S(2)}) copy-start(bf16[3,3,128,128]{3,2,1,0:T(8,128)(2,1)} %dw_ref.1) | copy-start | bytes 884740
  15.7 5.7 %copy-start.4 = (bf16[3,128,128]{2,1,0:T(8,128)(2,1)S(1)}, bf16[3,128,128]{2,1,0:T(8,128)(2,1)}, u32[]{:S(2)}) copy-start(bf16[3,128,128]{2,1,0:T(8,128)(2,1)} %tw_ref.1) | copy-start | bytes 294916

commit v4 on v3

--- a/solution.py
+++ b/solution.py
@@ -61,8 +61,8 @@
 
 
 def encode_kernel(
-    pos_ref, x_ref, up_ref, dn_ref, stats_ref, vec_ref, head_ref, keys_ref, slots_ref, cw_ref,
-    dw_ref, tw_ref, out_ref, raw, hid, skip, red,
+    pos_ref, x_ref, up_ref, dn_ref, stats_ref, vec_ref, mix_ref, keys_ref, slots_ref, cw_ref,
+    dw_ref, out_ref, raw, hid, skip, red,
 ):
     frames, rows, cols, channels = x_ref.shape
     pairs = cols // 2
@@ -171,20 +171,16 @@
         ],
         axis=0,
     )
-    mixing = jnp.concatenate([tw_ref[k] for k in range(3)], axis=0)
-    mixed = (matmul(taps, mixing) + vec_ref[4:5]).astype(BF16)
     width = channels // 4
-    latent = matmul_nt(mixed, head_ref[...]) + vec_ref[5:6]
+    latent = matmul(taps, mix_ref[...]) + vec_ref[4:5]
     spot = iota(latent.shape, 0) % spots
     corner = (spot // pairs) % 2 * 2 + spot % 2
     latent = jnp.where(iota(latent.shape, 1) // width == corner, latent, 0.0).astype(BF16)
 
     line = iota((out_ref.shape[0], spots), 0)
-    out = put_slots(slots_ref[...], out_ref.shape[0])
-    for l in range(lats):
-        chosen = onehot(line == keys_ref[l : l + 1])
-        out = out + matmul(chosen, latent[l * spots : (l + 1) * spots])
-    out_ref[...] = out.astype(BF16)
+    chosen = [onehot(line == keys_ref[l : l + 1]) for l in range(lats)]
+    out = matmul(jnp.concatenate(chosen, axis=1), latent)
+    out_ref[...] = (out + put_slots(slots_ref[...], out_ref.shape[0])).astype(BF16)
 
 
 def put_slots(slots, lines):
@@ -194,16 +190,24 @@
 
 
 def prep_kernel(*refs, pairs):
-    pos_ref, shard_ref, slot_ref, *line_refs, hw_ref = refs[:-4]
-    keys_ref, slots_ref, vec_ref, head_ref = refs[-4:]
-    copies = vec_ref.shape[1] // hw_ref.shape[0]
-    for i, ref in enumerate(line_refs):
-        row = ref[...]
-        if row.shape[1] < vec_ref.shape[1]:
-            row = jnp.concatenate([row] * copies, axis=1)
-        vec_ref[i : i + 1] = row
-    vec_ref[len(line_refs) :] = jnp.zeros((8 - len(line_refs), vec_ref.shape[1]), F32)
-    head_ref[...] = jnp.concatenate([hw_ref[...]] * copies, axis=0)
+    pos_ref, shard_ref, slot_ref, *line_refs, hw_ref, tw_ref = refs[:-4]
+    keys_ref, slots_ref, vec_ref, mix_ref = refs[-4:]
+    for i, ref in enumerate(line_refs[:4]):
+        vec_ref[i : i + 1] = ref[...]
+    channels = vec_ref.shape[1]
+    copies = channels // hw_ref.shape[0]
+    head = jnp.concatenate([hw_ref[...]] * copies, axis=0)
+    for k in range(3):
+        mix_ref[k * channels : (k + 1) * channels] = matmul_nt(tw_ref[k], head).astype(BF16)
+    time_bias = lax.dot_general(
+        jnp.broadcast_to(line_refs[4][...], (8, channels)),
+        head.astype(F32),
+        (((1,), (1,)), ((), ())),
+        precision=lax.Precision.HIGHEST,
+        preferred_element_type=F32,
+    )
+    head_bias = jnp.concatenate([line_refs[5][...]] * copies, axis=1)
+    vec_ref[4:] = jnp.broadcast_to(time_bias[:1] + head_bias, (4, channels))
     lats, _, tiles = shard_ref.shape
     shards, channels = slots_ref.shape
     spots = keys_ref.shape[1]
@@ -297,21 +301,21 @@
             jax.ShapeDtypeStruct((8, rows // 2 * pairs), jnp.int32),
             jax.ShapeDtypeStruct((shards, channels), BF16),
             jax.ShapeDtypeStruct((8, channels), F32),
-            jax.ShapeDtypeStruct((channels, channels), BF16),
+            jax.ShapeDtypeStruct((3 * channels, channels), BF16),
         ),
-        in_specs=[pl.BlockSpec(memory_space=pltpu.SMEM), *vmem(9)],
+        in_specs=[pl.BlockSpec(memory_space=pltpu.SMEM), *vmem(10)],
         out_specs=tuple(vmem(4)),
         compiler_params=pltpu.CompilerParams(vmem_limit_bytes=4 << 20),
         cost_estimate=pl.CostEstimate(flops=20_000_000_000, bytes_accessed=0, transcendentals=0),
         name="prep",
-    )(position, tile_shard.transpose(1, 0, 2), tile_slot.transpose(1, 0, 2), *lines, head_weight.T)
-    weights = (conv_weight, down_weight, time_weight)
+    )(position, tile_shard.transpose(1, 0, 2), tile_slot.transpose(1, 0, 2), *lines, head_weight.T, time_weight)
+    weights = (conv_weight, down_weight)
     outgoing = pl.pallas_call(
         encode_kernel,
         out_shape=jax.ShapeDtypeStruct((shards * PACK, channels), BF16),
         in_specs=[
             pl.BlockSpec(memory_space=pltpu.SMEM),
-            *vmem(11),
+            *vmem(10),
         ],
         out_specs=pl.BlockSpec(memory_space=pltpu.VMEM),
         scratch_shapes=[

time: 58 us -> 57.8 us (level)
  no operation moved by 1% of the time
where the time goes in v4:
time: 57.8 us; the launch traced here: 57.5 us
  blocking collectives  30.8 us (53%)
  starting transfers between devices  12.9 us (22%)
  Pallas kernels  6.72 us (12%)
  waiting for transfers between devices  5.17 us (9%)
  local copies, waits for them, and re-layouts  1.81 us (3%)
    all_to_all x1, blocking collectives, local(): lax.all_to_all(outgoing.reshape(shards, PACK, channels), 'clip', split_ax...  30.8 us
    all_to_all x1, starting transfers between devices, local(): lax.all_to_all(stats, 'frame', split_axis=0, concat_axis=0, tiled=True)  7.55 us
    all_to_all x1, waiting for transfers between devices, local(): lax.all_to_all(stats, 'frame', split_axis=0, concat_axis=0, tiled=True)  5.16 us
    pallas_call x1, Pallas kernels, local(): pl.pallas_call(encode_kernel, out_shape=jax.ShapeDtypeStruct((shards * PA...  4.39 us
    ppermute x1, starting transfers between devices, local(): lax.ppermute(tail, 'frame', [(i, i + 1) for i in range(devices - 1)])  4.02 us
    unnamed x28, local copies, waits for them, and re-layouts  1.81 us
    ppermute x1, starting transfers between devices, local(): lax.ppermute(head, 'frame', [(i + 1, i) for i in range(devices - 1)])  1.29 us
  transfers between devices with their start and end apart: 3, of which 1 were waited for; matrix products, arithmetic and copies ran while one was open for 0% of the time, Pallas kernels for 1%

profile of v4, /device:TPU:1, one launch (start us, length us, event | category | flops | bytes accessed | tf_op | source)
XLA Modules:
  0.0 57.5 jit_solution(13318862388995626277)
XLA Ops:
  0.0 1.1 %copy-done = bf16[1,5,8,64,128]{4,3,2,1,0:T(8,128)(2,1)S(1)} copy-done((bf16[1,5,8,64,128]{4,3,2,1,0:T(8,128)(2,1)S(1)}, bf16[1,5,8,64,128]{4,3,2,1,0:T(8,128)(2,1)}, u32[]{:S(2)}) %copy-start) | copy-done | bytes 655384
  1.1 0.9 %stats.1 = (f32[16,2,128]{2,1,0:T(2,128)}, bf16[5,1,64,128]{3,2,1,0:T(8,128)(2,1)S(1)}, bf16[5,2,64,128]{3,2,1,0:T(8,128)(2,1)S(1)}) custom-call(bf16[5,8,64,128]{3,2,1,0:T(8,128)(2,1)S(1)} %bitcast.14), custom_call_target="tpu_custom_call" | custom-call | tf_op jit(solution)/shard_map/stats/pallas_call | solution.py:278
  2.0 4.0 %collective-permute-start = (bf16[5,1,64,128]{3,2,1,0:T(8,128)(2,1)S(1)}, bf16[5,1,64,128]{3,2,1,0:T(8,128)(2,1)S(1)}, u32[]{:S(2)}, u32[]{:S(2)}) collective-permute-start(bf16[5,1,64,128]{3,2,1,0:T(8,128)(2,1)S(1)} %get-tuple-element.12), channel_id=1, source_target_pairs={{0,1},{1,2},{2,3},{3,4},{4,5},{5,6},{6,7},{7,8},{8,9},{9,10},{10,1... | collective-permute-start | bytes 245768 | tf_op jit(solution)/shard_map/ppermute | solution.py:291
  6.1 1.3 %collective-permute-start.1 = (bf16[5,2,64,128]{3,2,1,0:T(8,128)(2,1)S(1)}, bf16[5,2,64,128]{3,2,1,0:T(8,128)(2,1)S(1)}, u32[]{:S(2)}, u32[]{:S(2)}) collective-permute-start(bf16[5,2,64,128]{3,2,1,0:T(8,128)(2,1)S(1)} %get-tuple-element.13), channel_id=1, source_target_pairs={{1,0},{2,1},{3,2},{4,3},{5,4},{6,5},{7,6},{8,7},{9,8},{10,9},{11,1... | collective-permute-start | bytes 491528 | tf_op jit(solution)/shard_map/ppermute | solution.py:292
  7.4 7.6 %all-to-all-start = ((f32[16,2,128]{2,1,0:T(2,128)}), f32[16,2,128]{2,1,0:T(2,128)S(1)}, u32[]{:S(2)}, u32[]{:S(2)}) async-start(f32[16,2,128]{2,1,0:T(2,128)} %get-tuple-element.14), calls=%async_computation | async-start | bytes 32768 | tf_op jit(solution)/shard_map/all_to_all | solution.py:290
  14.9 0.0 copy-start.5
  14.9 0.0 copy-start.9
  14.9 0.0 copy-start.10
  15.0 0.0 copy-start.11
  15.0 0.0 copy-start.12
  15.0 0.0 copy-start.13
  15.0 0.0 copy-start.6
  15.0 0.0 copy-start.7
  15.0 0.0 copy-start.8
  15.0 0.6 %copy-done.5 = bf16[128,32]{0,1:T(8,128)(2,1)S(1)} copy-done((bf16[128,32]{0,1:T(8,128)(2,1)S(1)}, bf16[128,32]{0,1:T(8,128)(2,1)}, u32[]{:S(2)}) %copy-start.5) | copy-done | bytes 8216
  15.6 0.0 copy-done.12
  15.6 0.0 copy-done.13
  15.7 0.0 copy-done.6
  15.7 0.0 copy-done.7
  15.7 0.5 prep.1
  16.2 5.2 %all-to-all-done.stats_ref = f32[16,2,128]{2,1,0:T(2,128)S(1)} async-done(((f32[16,2,128]{2,1,0:T(2,128)}), f32[16,2,128]{2,1,0:T(2,128)S(1)}, u32[]{:S(2)}, u32[]{:S(2)}) %all-to-all-start) | async-done | bytes 16416 | tf_op jit(solution)/shard_map/all_to_all | solution.py:290
  21.4 4.4 %encode.1 = bf16[256,128]{1,0:T(8,128)(2,1)S(1)} custom-call(s32[1]{0:T(128)} %bitcast.refs_0_.pos_ref, bf16[5,8,64,128]{3,2,1,0:T(8,128)(2,1)S(1)} %bitcast.15, bf16[5,1,64,128]{3,2,1,0:T(8,128)(2,1)S(1)} %collective-permute-done.up_ref, bf16[5,2,64,128]{3,2,1,0:T(8,128)(2,1)S(1)} %collective-permute-done.1.dn_ref, ...), custom_call_target="tpu_custom_call" | custom-call | tf_op jit(solution)/shard_map/encode/pallas_call | solution.py:313
  25.8 30.8 %all_to_all.10 = bf16[32,8,128]{2,1,0:T(8,128)(2,1)S(1)} all-to-all(bf16[32,8,128]{2,1,0:T(8,128)(2,1)S(1)} %bitcast.16), channel_id=1, replica_groups=mesh['clip'=32,'frame'=16] {'clip'}, dimensions={0} | all-to-all | bytes 131072 | tf_op jit(solution)/shard_map/all_to_all | solution.py:332
  56.6 0.9 %place.1 = bf16[192,128]{1,0:T(8,128)(2,1)} custom-call(bf16[256,128]{1,0:T(8,128)(2,1)S(1)} %bitcast.17), custom_call_target="tpu_custom_call" | custom-call | tf_op jit(solution)/shard_map/place/pallas_call | solution.py:335
  (15 shorter events, 0.0 us)
Async XLA Ops:
  0.0 1.1 %copy-start = (bf16[1,5,8,64,128]{4,3,2,1,0:T(8,128)(2,1)S(1)}, bf16[1,5,8,64,128]{4,3,2,1,0:T(8,128)(2,1)}, u32[]{:S(2)}) copy-start(bf16[1,5,8,64,128]{4,3,2,1,0:T(8,128)(2,1)} %param.13) | copy-start | bytes 1966084
  1.1 13.9 %copy-start.4 = (bf16[3,128,128]{2,1,0:T(8,128)(2,1)S(1)}, bf16[3,128,128]{2,1,0:T(8,128)(2,1)}, u32[]{:S(2)}) copy-start(bf16[3,128,128]{2,1,0:T(8,128)(2,1)} %refs_10_.1) | copy-start | bytes 294916
  2.0 19.3 %collective-permute-start = (bf16[5,1,64,128]{3,2,1,0:T(8,128)(2,1)S(1)}, bf16[5,1,64,128]{3,2,1,0:T(8,128)(2,1)S(1)}, u32[]{:S(2)}, u32[]{:S(2)}) collective-permute-start(bf16[5,1,64,128]{3,2,1,0:T(8,128)(2,1)S(1)} %get-tuple-element.12), channel_id=1, source_target_pairs={{0,1},{1,2},{2,3},{3,4},{4,5},{5,6},{6,7},{7,8},{8,9},{9,10},{10,1... | collective-permute-start | bytes 245768 | tf_op jit(solution)/shard_map/ppermute | solution.py:291
  6.1 15.3 %collective-permute-start.1 = (bf16[5,2,64,128]{3,2,1,0:T(8,128)(2,1)S(1)}, bf16[5,2,64,128]{3,2,1,0:T(8,128)(2,1)S(1)}, u32[]{:S(2)}, u32[]{:S(2)}) collective-permute-start(bf16[5,2,64,128]{3,2,1,0:T(8,128)(2,1)S(1)} %get-tuple-element.13), channel_id=1, source_target_pairs={{1,0},{2,1},{3,2},{4,3},{5,4},{6,5},{7,6},{8,7},{9,8},{10,9},{11,1... | collective-permute-start | bytes 491528 | tf_op jit(solution)/shard_map/ppermute | solution.py:292
  7.4 14.0 %all-to-all-start = ((f32[16,2,128]{2,1,0:T(2,128)}), f32[16,2,128]{2,1,0:T(2,128)S(1)}, u32[]{:S(2)}, u32[]{:S(2)}) async-start(f32[16,2,128]{2,1,0:T(2,128)} %get-tuple-element.14), calls=%async_computation | async-start | bytes 32768 | tf_op jit(solution)/shard_map/all_to_all | solution.py:290
  14.9 0.7 %copy-start.5 = (bf16[128,32]{0,1:T(8,128)(2,1)S(1)}, bf16[128,32]{0,1:T(8,128)(2,1)}, u32[]{:S(2)}) copy-start(bf16[128,32]{0,1:T(8,128)(2,1)} %param.22) | copy-start | bytes 24580
  14.9 0.7 %copy-start.9 = (f32[128]{0:T(128)S(1)}, f32[128]{0:T(128)}, u32[]{:S(2)}) copy-start(f32[128]{0:T(128)} %param.15) | copy-start | bytes 1540
  14.9 0.7 %copy-start.10 = (f32[128]{0:T(128)S(1)}, f32[128]{0:T(128)}, u32[]{:S(2)}) copy-start(f32[128]{0:T(128)} %param.17) | copy-start | bytes 1540
  15.0 0.7 %copy-start.11 = (f32[128]{0:T(128)S(1)}, f32[128]{0:T(128)}, u32[]{:S(2)}) copy-start(f32[128]{0:T(128)} %param.19) | copy-start | bytes 1540
  15.0 0.7 %copy-start.12 = (f32[128]{0:T(128)S(1)}, f32[128]{0:T(128)}, u32[]{:S(2)}) copy-start(f32[128]{0:T(128)} %param.21) | copy-start | bytes 1540
  15.0 0.7 %copy-start.13 = (f32[32]{0:T(128)S(1)}, f32[32]{0:T(128)}, u32[]{:S(2)}) copy-start(f32[32]{0:T(128)} %param.23) | copy-start | bytes 388
  15.0 0.7 %copy-start.6 = (s32[1,3,32]{2,0,1:T(1,128)S(1)}, s32[1,3,32]{2,0,1:T(1,128)}, u32[]{:S(2)}) copy-start(s32[1,3,32]{2,0,1:T(1,128)} %param.24) | copy-start | bytes 1156
  15.0 0.7 %copy-start.7 = (s32[1,3,32]{2,0,1:T(1,128)S(1)}, s32[1,3,32]{2,0,1:T(1,128)}, u32[]{:S(2)}) copy-start(s32[1,3,32]{2,0,1:T(1,128)} %param.25) | copy-start | bytes 1156
  15.0 0.7 %copy-start.8 = (f32[128]{0:T(128)S(1)}, f32[128]{0:T(128)}, u32[]{:S(2)}) copy-start(f32[128]{0:T(128)} %param.14) | copy-start | bytes 1540
  15.7 5.7 %copy-start.1 = (bf16[1,5,8,64,128]{4,3,2,1,0:T(8,128)(2,1)S(1)}, bf16[1,5,8,64,128]{4,3,2,1,0:T(8,128)(2,1)}, u32[]{:S(2)}) copy-start(bf16[1,5,8,64,128]{4,3,2,1,0:T(8,128)(2,1)} %param.13) | copy-start | bytes 1966084
  15.7 5.7 %copy-start.2 = (bf16[3,3,3,128,128]{4,3,2,1,0:T(8,128)(2,1)S(1)}, bf16[3,3,3,128,128]{4,3,2,1,0:T(8,128)(2,1)}, u32[]{:S(2)}) copy-start(bf16[3,3,3,128,128]{4,3,2,1,0:T(8,128)(2,1)} %cw_ref.1) | copy-start | bytes 2654212
  15.7 5.7 %copy-start.3 = (bf16[3,3,128,128]{3,2,1,0:T(8,128)(2,1)S(1)}, bf16[3,3,128,128]{3,2,1,0:T(8,128)(2,1)}, u32[]{:S(2)}) copy-start(bf16[3,3,128,128]{3,2,1,0:T(8,128)(2,1)} %dw_ref.1) | copy-start | bytes 884740

commit v5 on v3

--- a/solution.py
+++ b/solution.py
@@ -180,11 +180,9 @@
     latent = jnp.where(iota(latent.shape, 1) // width == corner, latent, 0.0).astype(BF16)
 
     line = iota((out_ref.shape[0], spots), 0)
-    out = put_slots(slots_ref[...], out_ref.shape[0])
-    for l in range(lats):
-        chosen = onehot(line == keys_ref[l : l + 1])
-        out = out + matmul(chosen, latent[l * spots : (l + 1) * spots])
-    out_ref[...] = out.astype(BF16)
+    chosen = [onehot(line == keys_ref[l : l + 1]) for l in range(lats)]
+    out = matmul(jnp.concatenate(chosen, axis=1), latent)
+    out_ref[...] = (out + put_slots(slots_ref[...], out_ref.shape[0])).astype(BF16)
 
 
 def put_slots(slots, lines):

time: 58 us -> 57.9 us (level)
  no operation moved by 1% of the time
where the time goes in v5:
time: 57.9 us; the launch traced here: 57.6 us
  blocking collectives  30.8 us (53%)
  starting transfers between devices  12.9 us (22%)
  Pallas kernels  6.8 us (12%)
  waiting for transfers between devices  5.18 us (9%)
  local copies, waits for them, and re-layouts  1.83 us (3%)
    all_to_all x1, blocking collectives, local(): lax.all_to_all(outgoing.reshape(shards, PACK, channels), 'clip', split_ax...  30.8 us
    all_to_all x1, starting transfers between devices, local(): lax.all_to_all(stats, 'frame', split_axis=0, concat_axis=0, tiled=True)  7.55 us
    all_to_all x1, waiting for transfers between devices, local(): lax.all_to_all(stats, 'frame', split_axis=0, concat_axis=0, tiled=True)  5.18 us
    pallas_call x1, Pallas kernels, local(): pl.pallas_call(encode_kernel, out_shape=jax.ShapeDtypeStruct((shards * PA...  4.49 us
    ppermute x1, starting transfers between devices, local(): lax.ppermute(tail, 'frame', [(i, i + 1) for i in range(devices - 1)])  4.02 us
    unnamed x28, local copies, waits for them, and re-layouts  1.83 us
    ppermute x1, starting transfers between devices, local(): lax.ppermute(head, 'frame', [(i + 1, i) for i in range(devices - 1)])  1.29 us
  transfers between devices with their start and end apart: 3, of which 1 were waited for; matrix products, arithmetic and copies ran while one was open for 0% of the time, Pallas kernels for 1%

profile of v5, /device:TPU:1, one launch (start us, length us, event | category | flops | bytes accessed | tf_op | source)
XLA Modules:
  0.0 57.6 jit_solution(16584867538962202448)
XLA Ops:
  0.0 1.1 %copy-done = bf16[1,5,8,64,128]{4,3,2,1,0:T(8,128)(2,1)S(1)} copy-done((bf16[1,5,8,64,128]{4,3,2,1,0:T(8,128)(2,1)S(1)}, bf16[1,5,8,64,128]{4,3,2,1,0:T(8,128)(2,1)}, u32[]{:S(2)}) %copy-start) | copy-done | bytes 655384
  1.1 0.9 %stats.1 = (f32[16,2,128]{2,1,0:T(2,128)}, bf16[5,1,64,128]{3,2,1,0:T(8,128)(2,1)S(1)}, bf16[5,2,64,128]{3,2,1,0:T(8,128)(2,1)S(1)}) custom-call(bf16[5,8,64,128]{3,2,1,0:T(8,128)(2,1)S(1)} %bitcast.14), custom_call_target="tpu_custom_call" | custom-call | tf_op jit(solution)/shard_map/stats/pallas_call | solution.py:272
  2.0 4.0 %collective-permute-start = (bf16[5,1,64,128]{3,2,1,0:T(8,128)(2,1)S(1)}, bf16[5,1,64,128]{3,2,1,0:T(8,128)(2,1)S(1)}, u32[]{:S(2)}, u32[]{:S(2)}) collective-permute-start(bf16[5,1,64,128]{3,2,1,0:T(8,128)(2,1)S(1)} %get-tuple-element.12), channel_id=1, source_target_pairs={{0,1},{1,2},{2,3},{3,4},{4,5},{5,6},{6,7},{7,8},{8,9},{9,10},{10,1... | collective-permute-start | bytes 245768 | tf_op jit(solution)/shard_map/ppermute | solution.py:285
  6.1 1.3 %collective-permute-start.1 = (bf16[5,2,64,128]{3,2,1,0:T(8,128)(2,1)S(1)}, bf16[5,2,64,128]{3,2,1,0:T(8,128)(2,1)S(1)}, u32[]{:S(2)}, u32[]{:S(2)}) collective-permute-start(bf16[5,2,64,128]{3,2,1,0:T(8,128)(2,1)S(1)} %get-tuple-element.13), channel_id=1, source_target_pairs={{1,0},{2,1},{3,2},{4,3},{5,4},{6,5},{7,6},{8,7},{9,8},{10,9},{11,1... | collective-permute-start | bytes 491528 | tf_op jit(solution)/shard_map/ppermute | solution.py:286
  7.4 7.6 %all-to-all-start = ((f32[16,2,128]{2,1,0:T(2,128)}), f32[16,2,128]{2,1,0:T(2,128)S(1)}, u32[]{:S(2)}, u32[]{:S(2)}) async-start(f32[16,2,128]{2,1,0:T(2,128)} %get-tuple-element.14), calls=%async_computation | async-start | bytes 32768 | tf_op jit(solution)/shard_map/all_to_all | solution.py:284
  14.9 0.0 copy-start.5
  14.9 0.0 copy-start.9
  14.9 0.0 copy-start.10
  15.0 0.0 copy-start.11
  15.0 0.0 copy-start.12
  15.0 0.0 copy-start.13
  15.0 0.0 copy-start.6
  15.0 0.0 copy-start.7
  15.0 0.0 copy-start.8
  15.0 0.6 %copy-done.5 = bf16[128,32]{0,1:T(8,128)(2,1)S(1)} copy-done((bf16[128,32]{0,1:T(8,128)(2,1)S(1)}, bf16[128,32]{0,1:T(8,128)(2,1)}, u32[]{:S(2)}) %copy-start.5) | copy-done | bytes 8216
  15.6 0.0 copy-done.12
  15.6 0.0 copy-done.13
  15.7 0.0 copy-done.6
  15.7 0.0 copy-done.7
  15.7 0.4 prep.1
  16.2 5.2 %all-to-all-done.stats_ref = f32[16,2,128]{2,1,0:T(2,128)S(1)} async-done(((f32[16,2,128]{2,1,0:T(2,128)}), f32[16,2,128]{2,1,0:T(2,128)S(1)}, u32[]{:S(2)}, u32[]{:S(2)}) %all-to-all-start) | async-done | bytes 16416 | tf_op jit(solution)/shard_map/all_to_all | solution.py:284
  21.4 4.5 %encode.1 = bf16[256,128]{1,0:T(8,128)(2,1)S(1)} custom-call(s32[1]{0:T(128)} %bitcast.refs_0_.pos_ref, bf16[5,8,64,128]{3,2,1,0:T(8,128)(2,1)S(1)} %bitcast.15, bf16[5,1,64,128]{3,2,1,0:T(8,128)(2,1)S(1)} %collective-permute-done.up_ref, bf16[5,2,64,128]{3,2,1,0:T(8,128)(2,1)S(1)} %collective-permute-done.1.dn_ref, ...), custom_call_target="tpu_custom_call" | custom-call | tf_op jit(solution)/shard_map/encode/pallas_call | solution.py:307
  25.9 30.8 %all_to_all.10 = bf16[32,8,128]{2,1,0:T(8,128)(2,1)S(1)} all-to-all(bf16[32,8,128]{2,1,0:T(8,128)(2,1)S(1)} %bitcast.16), channel_id=1, replica_groups=mesh['clip'=32,'frame'=16] {'clip'}, dimensions={0} | all-to-all | bytes 131072 | tf_op jit(solution)/shard_map/all_to_all | solution.py:326
  56.7 0.9 %place.1 = bf16[192,128]{1,0:T(8,128)(2,1)} custom-call(bf16[256,128]{1,0:T(8,128)(2,1)S(1)} %bitcast.17), custom_call_target="tpu_custom_call" | custom-call | tf_op jit(solution)/shard_map/place/pallas_call | solution.py:329
  (15 shorter events, 0.0 us)
Async XLA Ops:
  0.0 1.1 %copy-start = (bf16[1,5,8,64,128]{4,3,2,1,0:T(8,128)(2,1)S(1)}, bf16[1,5,8,64,128]{4,3,2,1,0:T(8,128)(2,1)}, u32[]{:S(2)}) copy-start(bf16[1,5,8,64,128]{4,3,2,1,0:T(8,128)(2,1)} %param.13) | copy-start | bytes 1966084
  2.0 19.3 %collective-permute-start = (bf16[5,1,64,128]{3,2,1,0:T(8,128)(2,1)S(1)}, bf16[5,1,64,128]{3,2,1,0:T(8,128)(2,1)S(1)}, u32[]{:S(2)}, u32[]{:S(2)}) collective-permute-start(bf16[5,1,64,128]{3,2,1,0:T(8,128)(2,1)S(1)} %get-tuple-element.12), channel_id=1, source_target_pairs={{0,1},{1,2},{2,3},{3,4},{4,5},{5,6},{6,7},{7,8},{8,9},{9,10},{10,1... | collective-permute-start | bytes 245768 | tf_op jit(solution)/shard_map/ppermute | solution.py:285
  6.1 15.3 %collective-permute-start.1 = (bf16[5,2,64,128]{3,2,1,0:T(8,128)(2,1)S(1)}, bf16[5,2,64,128]{3,2,1,0:T(8,128)(2,1)S(1)}, u32[]{:S(2)}, u32[]{:S(2)}) collective-permute-start(bf16[5,2,64,128]{3,2,1,0:T(8,128)(2,1)S(1)} %get-tuple-element.13), channel_id=1, source_target_pairs={{1,0},{2,1},{3,2},{4,3},{5,4},{6,5},{7,6},{8,7},{9,8},{10,9},{11,1... | collective-permute-start | bytes 491528 | tf_op jit(solution)/shard_map/ppermute | solution.py:286
  7.4 14.0 %all-to-all-start = ((f32[16,2,128]{2,1,0:T(2,128)}), f32[16,2,128]{2,1,0:T(2,128)S(1)}, u32[]{:S(2)}, u32[]{:S(2)}) async-start(f32[16,2,128]{2,1,0:T(2,128)} %get-tuple-element.14), calls=%async_computation | async-start | bytes 32768 | tf_op jit(solution)/shard_map/all_to_all | solution.py:284
  14.9 0.7 %copy-start.5 = (bf16[128,32]{0,1:T(8,128)(2,1)S(1)}, bf16[128,32]{0,1:T(8,128)(2,1)}, u32[]{:S(2)}) copy-start(bf16[128,32]{0,1:T(8,128)(2,1)} %param.22) | copy-start | bytes 24580
  14.9 0.7 %copy-start.9 = (f32[128]{0:T(128)S(1)}, f32[128]{0:T(128)}, u32[]{:S(2)}) copy-start(f32[128]{0:T(128)} %param.15) | copy-start | bytes 1540
  14.9 0.7 %copy-start.10 = (f32[128]{0:T(128)S(1)}, f32[128]{0:T(128)}, u32[]{:S(2)}) copy-start(f32[128]{0:T(128)} %param.17) | copy-start | bytes 1540
  15.0 0.7 %copy-start.11 = (f32[128]{0:T(128)S(1)}, f32[128]{0:T(128)}, u32[]{:S(2)}) copy-start(f32[128]{0:T(128)} %param.19) | copy-start | bytes 1540
  15.0 0.7 %copy-start.12 = (f32[128]{0:T(128)S(1)}, f32[128]{0:T(128)}, u32[]{:S(2)}) copy-start(f32[128]{0:T(128)} %param.21) | copy-start | bytes 1540
  15.0 0.7 %copy-start.13 = (f32[32]{0:T(128)S(1)}, f32[32]{0:T(128)}, u32[]{:S(2)}) copy-start(f32[32]{0:T(128)} %param.23) | copy-start | bytes 388
  15.0 0.7 %copy-start.6 = (s32[1,3,32]{2,0,1:T(1,128)S(1)}, s32[1,3,32]{2,0,1:T(1,128)}, u32[]{:S(2)}) copy-start(s32[1,3,32]{2,0,1:T(1,128)} %param.24) | copy-start | bytes 1156
  15.0 0.7 %copy-start.7 = (s32[1,3,32]{2,0,1:T(1,128)S(1)}, s32[1,3,32]{2,0,1:T(1,128)}, u32[]{:S(2)}) copy-start(s32[1,3,32]{2,0,1:T(1,128)} %param.25) | copy-start | bytes 1156
  15.0 0.7 %copy-start.8 = (f32[128]{0:T(128)S(1)}, f32[128]{0:T(128)}, u32[]{:S(2)}) copy-start(f32[128]{0:T(128)} %param.14) | copy-start | bytes 1540
  15.7 5.7 %copy-start.1 = (bf16[1,5,8,64,128]{4,3,2,1,0:T(8,128)(2,1)S(1)}, bf16[1,5,8,64,128]{4,3,2,1,0:T(8,128)(2,1)}, u32[]{:S(2)}) copy-start(bf16[1,5,8,64,128]{4,3,2,1,0:T(8,128)(2,1)} %param.13) | copy-start | bytes 1966084
  15.7 5.7 %copy-start.2 = (bf16[3,3,3,128,128]{4,3,2,1,0:T(8,128)(2,1)S(1)}, bf16[3,3,3,128,128]{4,3,2,1,0:T(8,128)(2,1)}, u32[]{:S(2)}) copy-start(bf16[3,3,3,128,128]{4,3,2,1,0:T(8,128)(2,1)} %cw_ref.1) | copy-start | bytes 2654212
  15.7 5.7 %copy-start.3 = (bf16[3,3,128,128]{3,2,1,0:T(8,128)(2,1)S(1)}, bf16[3,3,128,128]{3,2,1,0:T(8,128)(2,1)}, u32[]{:S(2)}) copy-start(bf16[3,3,128,128]{3,2,1,0:T(8,128)(2,1)} %dw_ref.1) | copy-start | bytes 884740
  15.7 5.7 %copy-start.4 = (bf16[3,128,128]{2,1,0:T(8,128)(2,1)S(1)}, bf16[3,128,128]{2,1,0:T(8,128)(2,1)}, u32[]{:S(2)}) copy-start(bf16[3,128,128]{2,1,0:T(8,128)(2,1)} %tw_ref.1) | copy-start | bytes 294916

commit v6 on v5

--- a/solution.py
+++ b/solution.py
@@ -30,22 +30,31 @@
     return lax.dot_general(lhs, rhs, (((1,), (1,)), ((), ())), preferred_element_type=F32)
 
 
-def stats_kernel(x_ref, stats_ref, tail_ref, head_ref):
+def stats_kernel(x_ref, stats_ref, tail_ref, head_ref, held, sems):
     frames, rows, cols, channels = x_ref.shape
-    count = frames * rows * cols
-
-    def over_all(change):
-        parts = [jnp.sum(change(x_ref[f].astype(F32)), axis=0) for f in range(frames)]
-        return jnp.sum(sum(parts), axis=0, keepdims=True)
-
-    total = over_all(lambda v: v)
-    mean = total / count
-    spread = over_all(lambda v: (v - mean) * (v - mean))
+    count = rows * cols
+    copies = [pltpu.make_async_copy(x_ref.at[f], held.at[f], sems.at[f]) for f in range(frames)]
+    for copy in copies:
+        copy.start()
+    totals, spreads = [], []
+    for f in range(frames):
+        copies[f].wait()
+        block = held[f].astype(F32)
+        total = jnp.sum(jnp.sum(block, axis=0), axis=0, keepdims=True)
+        off = block - total / count
+        totals.append(total)
+        spreads.append(jnp.sum(off * off, axis=0))
+        tail_ref[f] = held[f, rows - 1 :]
+        head_ref[f] = held[f, :2]
+    total = sum(totals)
+    mean = total / (count * frames)
+    spread = jnp.sum(sum(spreads), axis=0, keepdims=True)
+    for f in range(frames):
+        off = totals[f] / count - mean
+        spread = spread + count * (off * off)
     both = jnp.concatenate([total, spread], axis=0)
     for d in range(stats_ref.shape[0]):
         stats_ref[d] = both
-    tail_ref[...] = x_ref[:, rows - 1 :]
-    head_ref[...] = x_ref[:, :2]
 
 
 def over_group(values, width):
@@ -276,9 +285,13 @@
             jax.ShapeDtypeStruct((frames, 1, cols, channels), BF16),
             jax.ShapeDtypeStruct((frames, 2, cols, channels), BF16),
         ),
-        in_specs=vmem(1),
+        in_specs=[pl.BlockSpec(memory_space=pltpu.HBM)],
         out_specs=tuple(vmem(3)),
-        compiler_params=pltpu.CompilerParams(vmem_limit_bytes=8 << 20),
+        scratch_shapes=[
+            pltpu.VMEM((frames, rows, cols, channels), BF16),
+            pltpu.SemaphoreType.DMA((frames,)),
+        ],
+        compiler_params=pltpu.CompilerParams(vmem_limit_bytes=63 << 20),
         name="stats",
     )(activations)
     stats = lax.all_to_all(stats, "frame", split_axis=0, concat_axis=0, tiled=True)

time: 57.9 us -> 57.8 us (level)
  local copies, waits for them, and re-layouts: 1.83 us -> 0.74 us
  Pallas kernels: 6.8 us -> 7.78 us
    unnamed x28 -> x26, local copies, waits for them, and re-layouts: 1.83 us -> 0.74 us
    pallas_call x1, Pallas kernels: 0.93 us -> 1.9 us  [local(): pl.pallas_call(stats_kernel, out_shape=(jax.ShapeDtypeStruct((devices, 2,...]
where the time goes in v6:
time: 57.8 us; the launch traced here: 57.5 us
  blocking collectives  30.8 us (53%)
  starting transfers between devices  12.9 us (22%)
  Pallas kernels  7.78 us (13%)
  waiting for transfers between devices  5.18 us (9%)
  local copies, waits for them, and re-layouts  0.74 us (1%)
    all_to_all x1, blocking collectives, local(): lax.all_to_all(outgoing.reshape(shards, PACK, channels), 'clip', split_ax...  30.8 us
    all_to_all x1, starting transfers between devices, local(): lax.all_to_all(stats, 'frame', split_axis=0, concat_axis=0, tiled=True)  7.55 us
    all_to_all x1, waiting for transfers between devices, local(): lax.all_to_all(stats, 'frame', split_axis=0, concat_axis=0, tiled=True)  5.18 us
    pallas_call x1, Pallas kernels, local(): pl.pallas_call(encode_kernel, out_shape=jax.ShapeDtypeStruct((shards * PA...  4.51 us
    ppermute x1, starting transfers between devices, local(): lax.ppermute(tail, 'frame', [(i, i + 1) for i in range(devices - 1)])  4.03 us
    pallas_call x1, Pallas kernels, local(): pl.pallas_call(stats_kernel, out_shape=(jax.ShapeDtypeStruct((devices, 2,...  1.9 us
    ppermute x1, starting transfers between devices, local(): lax.ppermute(head, 'frame', [(i + 1, i) for i in range(devices - 1)])  1.29 us
  transfers between devices with their start and end apart: 3, of which 1 were waited for; matrix products, arithmetic and copies ran while one was open for 0% of the time, Pallas kernels for 1%

profile of v6, /device:TPU:1, one launch (start us, length us, event | category | flops | bytes accessed | tf_op | source)
XLA Modules:
  0.0 57.5 jit_solution(5505757219979414952)
XLA Ops:
  0.0 1.9 %stats.1 = (f32[16,2,128]{2,1,0:T(2,128)}, bf16[5,1,64,128]{3,2,1,0:T(8,128)(2,1)}, bf16[5,2,64,128]{3,2,1,0:T(8,128)(2,1)}) custom-call(bf16[5,8,64,128]{3,2,1,0:T(8,128)(2,1)} %bitcast.14), custom_call_target="tpu_custom_call" | custom-call | tf_op jit(solution)/shard_map/stats/pallas_call | solution.py:281
  1.9 4.0 %collective-permute-start = (bf16[5,1,64,128]{3,2,1,0:T(8,128)(2,1)}, bf16[5,1,64,128]{3,2,1,0:T(8,128)(2,1)S(1)}, u32[]{:S(2)}, u32[]{:S(2)}) collective-permute-start(bf16[5,1,64,128]{3,2,1,0:T(8,128)(2,1)} %get-tuple-element.12), channel_id=1, source_target_pairs={{0,1},{1,2},{2,3},{3,4},{4,5},{5,6},{6,7},{7,8},{8,9},{9,10},{10,1... | collective-permute-start | bytes 245768 | tf_op jit(solution)/shard_map/ppermute | solution.py:298
  6.0 1.3 %collective-permute-start.1 = (bf16[5,2,64,128]{3,2,1,0:T(8,128)(2,1)}, bf16[5,2,64,128]{3,2,1,0:T(8,128)(2,1)S(1)}, u32[]{:S(2)}, u32[]{:S(2)}) collective-permute-start(bf16[5,2,64,128]{3,2,1,0:T(8,128)(2,1)} %get-tuple-element.13), channel_id=1, source_target_pairs={{1,0},{2,1},{3,2},{4,3},{5,4},{6,5},{7,6},{8,7},{9,8},{10,9},{11,1... | collective-permute-start | bytes 491528 | tf_op jit(solution)/shard_map/ppermute | solution.py:299
  7.3 7.6 %all-to-all-start = ((f32[16,2,128]{2,1,0:T(2,128)}), f32[16,2,128]{2,1,0:T(2,128)S(1)}, u32[]{:S(2)}, u32[]{:S(2)}) async-start(f32[16,2,128]{2,1,0:T(2,128)} %get-tuple-element.14), calls=%async_computation | async-start | bytes 32768 | tf_op jit(solution)/shard_map/all_to_all | solution.py:297
  14.8 0.0 copy-start.4
  14.8 0.0 copy-start.8
  14.8 0.0 copy-start.9
  14.9 0.0 copy-start.10
  14.9 0.0 copy-start.11
  14.9 0.0 copy-start.12
  14.9 0.0 copy-start.5
  14.9 0.0 copy-start.6
  14.9 0.0 copy-start.7
  14.9 0.6 %copy-done.4 = bf16[128,32]{0,1:T(8,128)(2,1)S(1)} copy-done((bf16[128,32]{0,1:T(8,128)(2,1)S(1)}, bf16[128,32]{0,1:T(8,128)(2,1)}, u32[]{:S(2)}) %copy-start.4) | copy-done | bytes 8216
  15.5 0.0 copy-done.11
  15.5 0.0 copy-done.12
  15.6 0.0 copy-done.5
  15.6 0.0 copy-done.6
  15.6 0.0 copy-start.3
  15.6 0.4 prep.1
  16.1 5.2 %all-to-all-done.stats_ref = f32[16,2,128]{2,1,0:T(2,128)S(1)} async-done(((f32[16,2,128]{2,1,0:T(2,128)}), f32[16,2,128]{2,1,0:T(2,128)S(1)}, u32[]{:S(2)}, u32[]{:S(2)}) %all-to-all-start) | async-done | bytes 16416 | tf_op jit(solution)/shard_map/all_to_all | solution.py:297
  21.3 4.5 %encode.1 = bf16[256,128]{1,0:T(8,128)(2,1)S(1)} custom-call(s32[1]{0:T(128)} %bitcast.refs_0_.pos_ref, bf16[5,8,64,128]{3,2,1,0:T(8,128)(2,1)S(1)} %bitcast.15, bf16[5,1,64,128]{3,2,1,0:T(8,128)(2,1)S(1)} %collective-permute-done.up_ref, bf16[5,2,64,128]{3,2,1,0:T(8,128)(2,1)S(1)} %collective-permute-done.1.dn_ref, ...), custom_call_target="tpu_custom_call" | custom-call | tf_op jit(solution)/shard_map/encode/pallas_call | solution.py:320
  25.8 30.8 %all_to_all.10 = bf16[32,8,128]{2,1,0:T(8,128)(2,1)S(1)} all-to-all(bf16[32,8,128]{2,1,0:T(8,128)(2,1)S(1)} %bitcast.16), channel_id=1, replica_groups=mesh['clip'=32,'frame'=16] {'clip'}, dimensions={0} | all-to-all | bytes 131072 | tf_op jit(solution)/shard_map/all_to_all | solution.py:339
  56.6 0.9 %place.1 = bf16[192,128]{1,0:T(8,128)(2,1)} custom-call(bf16[256,128]{1,0:T(8,128)(2,1)S(1)} %bitcast.17), custom_call_target="tpu_custom_call" | custom-call | tf_op jit(solution)/shard_map/place/pallas_call | solution.py:342
  (13 shorter events, 0.0 us)
Async XLA Ops:
  1.9 19.4 %collective-permute-start = (bf16[5,1,64,128]{3,2,1,0:T(8,128)(2,1)}, bf16[5,1,64,128]{3,2,1,0:T(8,128)(2,1)S(1)}, u32[]{:S(2)}, u32[]{:S(2)}) collective-permute-start(bf16[5,1,64,128]{3,2,1,0:T(8,128)(2,1)} %get-tuple-element.12), channel_id=1, source_target_pairs={{0,1},{1,2},{2,3},{3,4},{4,5},{5,6},{6,7},{7,8},{8,9},{9,10},{10,1... | collective-permute-start | bytes 245768 | tf_op jit(solution)/shard_map/ppermute | solution.py:298
  6.0 15.3 %collective-permute-start.1 = (bf16[5,2,64,128]{3,2,1,0:T(8,128)(2,1)}, bf16[5,2,64,128]{3,2,1,0:T(8,128)(2,1)S(1)}, u32[]{:S(2)}, u32[]{:S(2)}) collective-permute-start(bf16[5,2,64,128]{3,2,1,0:T(8,128)(2,1)} %get-tuple-element.13), channel_id=1, source_target_pairs={{1,0},{2,1},{3,2},{4,3},{5,4},{6,5},{7,6},{8,7},{9,8},{10,9},{11,1... | collective-permute-start | bytes 491528 | tf_op jit(solution)/shard_map/ppermute | solution.py:299
  7.3 14.0 %all-to-all-start = ((f32[16,2,128]{2,1,0:T(2,128)}), f32[16,2,128]{2,1,0:T(2,128)S(1)}, u32[]{:S(2)}, u32[]{:S(2)}) async-start(f32[16,2,128]{2,1,0:T(2,128)} %get-tuple-element.14), calls=%async_computation | async-start | bytes 32768 | tf_op jit(solution)/shard_map/all_to_all | solution.py:297
  14.8 0.7 %copy-start.4 = (bf16[128,32]{0,1:T(8,128)(2,1)S(1)}, bf16[128,32]{0,1:T(8,128)(2,1)}, u32[]{:S(2)}) copy-start(bf16[128,32]{0,1:T(8,128)(2,1)} %param.22) | copy-start | bytes 24580
  14.8 0.7 %copy-start.8 = (f32[128]{0:T(128)S(1)}, f32[128]{0:T(128)}, u32[]{:S(2)}) copy-start(f32[128]{0:T(128)} %param.15) | copy-start | bytes 1540
  14.8 0.7 %copy-start.9 = (f32[128]{0:T(128)S(1)}, f32[128]{0:T(128)}, u32[]{:S(2)}) copy-start(f32[128]{0:T(128)} %param.17) | copy-start | bytes 1540
  14.9 0.7 %copy-start.10 = (f32[128]{0:T(128)S(1)}, f32[128]{0:T(128)}, u32[]{:S(2)}) copy-start(f32[128]{0:T(128)} %param.19) | copy-start | bytes 1540
  14.9 0.7 %copy-start.11 = (f32[128]{0:T(128)S(1)}, f32[128]{0:T(128)}, u32[]{:S(2)}) copy-start(f32[128]{0:T(128)} %param.21) | copy-start | bytes 1540
  14.9 0.7 %copy-start.12 = (f32[32]{0:T(128)S(1)}, f32[32]{0:T(128)}, u32[]{:S(2)}) copy-start(f32[32]{0:T(128)} %param.23) | copy-start | bytes 388
  14.9 0.7 %copy-start.5 = (s32[1,3,32]{2,0,1:T(1,128)S(1)}, s32[1,3,32]{2,0,1:T(1,128)}, u32[]{:S(2)}) copy-start(s32[1,3,32]{2,0,1:T(1,128)} %param.24) | copy-start | bytes 1156
  14.9 0.7 %copy-start.6 = (s32[1,3,32]{2,0,1:T(1,128)S(1)}, s32[1,3,32]{2,0,1:T(1,128)}, u32[]{:S(2)}) copy-start(s32[1,3,32]{2,0,1:T(1,128)} %param.25) | copy-start | bytes 1156
  14.9 0.7 %copy-start.7 = (f32[128]{0:T(128)S(1)}, f32[128]{0:T(128)}, u32[]{:S(2)}) copy-start(f32[128]{0:T(128)} %param.14) | copy-start | bytes 1540
  15.6 5.7 %copy-start = (bf16[1,5,8,64,128]{4,3,2,1,0:T(8,128)(2,1)S(1)}, bf16[1,5,8,64,128]{4,3,2,1,0:T(8,128)(2,1)}, u32[]{:S(2)}) copy-start(bf16[1,5,8,64,128]{4,3,2,1,0:T(8,128)(2,1)} %param.13) | copy-start | bytes 1966084
  15.6 5.7 %copy-start.1 = (bf16[3,3,3,128,128]{4,3,2,1,0:T(8,128)(2,1)S(1)}, bf16[3,3,3,128,128]{4,3,2,1,0:T(8,128)(2,1)}, u32[]{:S(2)}) copy-start(bf16[3,3,3,128,128]{4,3,2,1,0:T(8,128)(2,1)} %cw_ref.1) | copy-start | bytes 2654212
  15.6 5.7 %copy-start.2 = (bf16[3,3,128,128]{3,2,1,0:T(8,128)(2,1)S(1)}, bf16[3,3,128,128]{3,2,1,0:T(8,128)(2,1)}, u32[]{:S(2)}) copy-start(bf16[3,3,128,128]{3,2,1,0:T(8,128)(2,1)} %dw_ref.1) | copy-start | bytes 884740
  15.6 5.7 %copy-start.3 = (bf16[3,128,128]{2,1,0:T(8,128)(2,1)S(1)}, bf16[3,128,128]{2,1,0:T(8,128)(2,1)}, u32[]{:S(2)}) copy-start(bf16[3,128,128]{2,1,0:T(8,128)(2,1)} %tw_ref.1) | copy-start | bytes 294916
